TPU v7x, 32 devices: a whole 2x2x4 slice. The times are simulated.
32 devices in a mesh: dp: 2 (over y), ctx: 8 (over z, x), tp: 2 (over core).
Axes of the slice: x: 2, y: 2, z: 4, core: 2. Of those that a mesh axis runs over, the one named last changes fastest.
Arguments:
- inputs: bfloat16 [2, 1024, 768], P('dp', 'ctx'), may hold values from -6 to 6
- segments: int32 [2, 1024], P('dp', 'ctx'), may hold values from 0 to 2, as said below
- gain_one: float32 [768], replicated, may hold values from 0.5 to 1.5
- bias_one: float32 [768], replicated, may hold values from -1.5 to 1.5
- gain_two: float32 [768], replicated, may hold values from 0.5 to 1.5
- bias_two: float32 [768], replicated, may hold values from -1.5 to 1.5
- w_qkv: bfloat16 [768, 3, 768], P(('dp', 'ctx'), None, 'tp'), may hold values from -0.21875 to 0.21875
- b_qkv: float32 [3, 768], P(None, 'tp'), may hold values from -0.5 to 0.5
- w_out: bfloat16 [768, 768], P(('dp', 'ctx'), 'tp'), may hold values from -1.75 to 1.75
- out_bias: float32 [768], replicated, may hold values from -1.5 to 1.5
- w_up: bfloat16 [768, 3072], P(('dp', 'ctx'), 'tp'), may hold values from -0.21875 to 0.21875
- b_up: float32 [3072], P('tp'), may hold values from -1.5 to 1.5
- w_down: bfloat16 [768, 3072], P(('dp', 'ctx'), 'tp'), may hold values from -0.109375 to 0.109375
- cotangent: bfloat16 [2, 1024, 768], P('dp', 'ctx'), may hold values from -6 to 6
Outputs:
- output: float32 [2, 1024, 768], P('dp', 'ctx', 'tp')
- grad_inputs: float32 [2, 1024, 768], P('dp', 'ctx', 'tp')
- grad_gain_one: float32 [768], replicated
- grad_bias_one: float32 [768], replicated
- grad_gain_two: float32 [768], replicated
- grad_bias_two: float32 [768], replicated
- grad_w_qkv: float32 [768, 3, 768], P(('dp', 'ctx'), None, 'tp')
- grad_b_qkv: float32 [3, 768], P(None, 'tp')
- grad_w_out: float32 [768, 768], P(('dp', 'ctx'), 'tp')
- grad_out_bias: float32 [768], replicated
- grad_w_up: float32 [768, 3072], P(('dp', 'ctx'), 'tp')
- grad_b_up: float32 [3072], P('tp')
- grad_w_down: float32 [768, 3072], P(('dp', 'ctx'), 'tp')
Inputs may be any that keep to these rules, and one draw needn't show every extreme that they name: `segments`: in every row the segment numbers are 0, 1 and 2, all three present, never falling along the row; the first and the last segment each hold 1 to 64 tokens.
All inputs are finite; a program needn't handle non-finite values.
Results may differ from a plain program's by a relative error of at most 0.012.
Values may be sent and summed in bfloat16 or wider, within the bound.
A program may use at most 128 MiB of HBM per device.

v0:
```python
import math

import jax
import jax.numpy as jnp
from jax import lax
from jax.sharding import PartitionSpec as P

HD = 64
ROT = 16


NORM_EPSILON = 1e-05
NEG_LARGE = -1e30


def layer_norm(values, norm_gain, norm_bias):
    average = jnp.mean(values, axis=-1, keepdims=True)
    centered = values - average
    variance = jnp.mean(centered * centered, axis=-1, keepdims=True)
    return centered * lax.rsqrt(variance + NORM_EPSILON) * norm_gain + norm_bias


def angle_tables(first_row, length):
    positions = (first_row + jnp.arange(length)).astype(jnp.float32)
    frequency = 10000.0 ** (-(jnp.arange(ROT // 2).astype(jnp.float32) * 2.0 / ROT))
    angles = positions[:, None] * frequency[None, :]
    return (jnp.cos(angles)[:, None, :], jnp.sin(angles)[:, None, :])


def rotate(values, cosine_table, sine_table):
    half_rot = cosine_table.shape[-1]
    lower = values[..., :half_rot]
    upper = values[..., half_rot : 2 * half_rot]
    return jnp.concatenate(
        [
            lower * cosine_table - upper * sine_table,
            upper * cosine_table + lower * sine_table,
            values[..., 2 * half_rot :],
        ],
        axis=-1,
    )


def score_block(query_rows, key_block, key_seg, key_first, query_index, query_seg, softmax_scale):
    scores = (
        jnp.einsum("qhd,khd->qhk", query_rows, key_block, preferred_element_type=jnp.float32)
        * softmax_scale
    )
    key_index = key_first + jnp.arange(key_block.shape[0])
    allowed = (key_index[None, :] <= query_index[:, None]) & (
        key_seg[None, :] == query_seg[:, None]
    )
    return (scores, allowed[:, None, :])


def softmax_grads(grad_rows, log_total, grad_dots, value_block, scores, allowed):
    probability = jnp.where(allowed, jnp.exp(scores - log_total[..., None]), 0.0)
    grad_probs = jnp.einsum(
        "qhd,khd->qhk", grad_rows, value_block, preferred_element_type=jnp.float32
    )
    grad_scores = (probability * (grad_probs - grad_dots[..., None])).astype(jnp.bfloat16)
    return (probability.astype(jnp.bfloat16), grad_scores)


def on_device(
    inputs,
    segments,
    gain_one,
    bias_one,
    gain_two,
    bias_two,
    w_qkv,
    b_qkv,
    w_out,
    out_bias,
    w_up,
    b_up,
    w_down,
    cotangent,
):
    tokens = inputs[0].astype(jnp.float32)
    local_rows = tokens.shape[0]
    model_width = tokens.shape[1]
    share_width = model_width // lax.axis_size("tp")
    share_start = lax.axis_index("tp") * share_width
    offset_here = lax.axis_index("ctx") * local_rows
    query_index = offset_here + jnp.arange(local_rows)
    last_query = offset_here + local_rows - 1
    own_seg = segments[0].astype(jnp.bfloat16)
    qkv_all, out_all, up_all, down_all = (
        lax.all_gather(w_qkv, ("dp", "ctx"), axis=0, tiled=True),
        lax.all_gather(w_out, ("dp", "ctx"), axis=0, tiled=True),
        lax.all_gather(w_up, ("dp", "ctx"), axis=0, tiled=True),
        lax.all_gather(w_down, ("dp", "ctx"), axis=0, tiled=True),
    )
    norm_one = layer_norm(tokens, gain_one, bias_one).astype(jnp.bfloat16)
    norm_two = layer_norm(tokens, gain_two, bias_two).astype(jnp.bfloat16)
    projected = (
        jnp.einsum("td,dcm->tcm", norm_one, qkv_all, preferred_element_type=jnp.float32) + b_qkv
    )
    head_count = projected.shape[2] // HD
    cosine_table, sine_table = angle_tables(offset_here, local_rows)
    queries = rotate(
        projected[:, 0].reshape(local_rows, head_count, HD), cosine_table, sine_table
    ).astype(jnp.bfloat16)
    key_rows = rotate(
        projected[:, 1].reshape(local_rows, head_count, HD), cosine_table, sine_table
    ).astype(jnp.bfloat16)
    value_rows = projected[:, 2].reshape(local_rows, head_count, HD).astype(jnp.bfloat16)
    key_flat = key_rows.reshape(local_rows, -1)
    value_flat = value_rows.reshape(local_rows, -1)
    softmax_scale = 1.0 / math.sqrt(HD)
    zeros_rows = jnp.zeros((local_rows, head_count, HD), jnp.float32)
    initial = (
        jnp.full((local_rows, head_count), NEG_LARGE, jnp.float32),
        jnp.zeros((local_rows, head_count), jnp.float32),
        zeros_rows,
    )
    key_piece = lax.all_gather(key_flat, "ctx", axis=0, tiled=True)
    value_piece = lax.all_gather(value_flat, "ctx", axis=0, tiled=True)
    seg_piece = lax.all_gather(own_seg, "ctx", axis=0, tiled=True)
    piece_rows = key_piece.shape[0]
    piece_block = math.gcd(piece_rows, 512)
    piece_count = piece_rows // piece_block
    key_parts = key_piece.reshape(piece_count, piece_block, head_count, HD)
    value_parts = value_piece.reshape(piece_count, piece_block, head_count, HD)
    seg_parts = seg_piece.reshape(piece_count, piece_block)
    part_starts = piece_block * jnp.arange(piece_count)

    def visit_block(current, block_item):
        key_block, value_block, seg_block, key_first = block_item
        running_max, running_sum, running_out = current
        scores, allowed = score_block(
            queries, key_block, seg_block, key_first, query_index, own_seg, softmax_scale
        )
        block_max = jnp.max(jnp.where(allowed, scores, NEG_LARGE), axis=-1)
        new_max = jnp.maximum(running_max, block_max)
        probability = jnp.where(allowed, jnp.exp(scores - new_max[..., None]), 0.0)
        factor = jnp.exp(running_max - new_max)
        running_sum = running_sum * factor + jnp.sum(probability, axis=-1)
        running_out = running_out * factor[..., None] + jnp.einsum(
            "qhk,khd->qhd",
            probability.astype(jnp.bfloat16),
            value_block,
            preferred_element_type=jnp.float32,
        )
        return ((new_max, running_sum, running_out), None)

    def visit_all(current):
        return lax.scan(visit_block, current, (key_parts, value_parts, seg_parts, part_starts))[0]

    running_max, running_sum, running_out = lax.cond(
        jnp.int32(0) <= last_query, visit_all, lambda current: current, initial
    )
    attended = running_out / running_sum[..., None]
    log_total = running_max + jnp.log(running_sum)
    attended_low = attended.reshape(local_rows, -1).astype(jnp.bfloat16)
    contract_last = (((1,), (1,)), ((), ()))
    contract_rows = (((0,), (0,)), ((), ()))
    pre_gelu = jnp.dot(norm_two, up_all, preferred_element_type=jnp.float32) + b_up
    activated = jax.nn.gelu(pre_gelu, approximate=False).astype(jnp.bfloat16)
    branch_part = lax.dot_general(
        attended_low, out_all, contract_last, preferred_element_type=jnp.float32
    ) + lax.dot_general(activated, down_all, contract_last, preferred_element_type=jnp.float32)
    branch_share = lax.psum_scatter(
        branch_part.astype(jnp.bfloat16), "tp", scatter_dimension=1, tiled=True
    ).astype(jnp.float32)
    token_share = lax.dynamic_slice_in_dim(tokens, share_start, share_width, 1)
    bias_share = lax.dynamic_slice_in_dim(out_bias, share_start, share_width, 0)
    output = token_share + branch_share + bias_share
    grad_out = cotangent[0]
    grad_float = grad_out.astype(jnp.float32)
    grad_bias = jnp.sum(grad_float, axis=0)
    grad_attended = jnp.dot(grad_out, out_all, preferred_element_type=jnp.float32)
    grad_attended_low = grad_attended.astype(jnp.bfloat16).reshape(local_rows, head_count, HD)
    grad_activated = jnp.dot(grad_out, down_all, preferred_element_type=jnp.float32)
    gelu_pull = jax.vjp(lambda current: jax.nn.gelu(current, approximate=False), pre_gelu)[1]
    grad_pre = gelu_pull(grad_activated)[0].astype(jnp.bfloat16)
    grad_w_out = lax.dot_general(
        grad_out, attended_low, contract_rows, preferred_element_type=jnp.float32
    )
    grad_w_down = lax.dot_general(
        grad_out, activated, contract_rows, preferred_element_type=jnp.float32
    )
    grad_w_up = lax.dot_general(
        norm_two, grad_pre, contract_rows, preferred_element_type=jnp.float32
    )
    grad_b_up = jnp.sum(grad_pre.astype(jnp.float32), axis=0)
    grad_norm_two = lax.dot_general(
        grad_pre, up_all, contract_last, preferred_element_type=jnp.float32
    )
    grad_dots = jnp.sum(grad_attended_low.astype(jnp.float32) * attended, axis=-1)
    key_all, value_all, seg_all = (
        lax.all_gather(key_flat, "ctx", axis=0, tiled=True),
        lax.all_gather(value_flat, "ctx", axis=0, tiled=True),
        lax.all_gather(own_seg, "ctx", axis=0, tiled=True),
    )
    total_rows = key_all.shape[0]
    block_size = math.gcd(total_rows, 512)
    block_count = total_rows // block_size
    key_blocks = key_all.reshape(block_count, block_size, head_count, HD)
    value_blocks = value_all.reshape(block_count, block_size, head_count, HD)
    seg_blocks = seg_all.reshape(block_count, block_size)
    block_starts = block_size * jnp.arange(block_count)

    def visit_back(grad_query, block_item):
        key_block, value_block, seg_block, key_first = block_item

        def compute_block(grad_query):
            scores, allowed = score_block(
                queries, key_block, seg_block, key_first, query_index, own_seg, softmax_scale
            )
            prob_low, grad_scores = softmax_grads(
                grad_attended_low, log_total, grad_dots, value_block, scores, allowed
            )
            grad_query = grad_query + jnp.einsum(
                "qhk,khd->qhd", grad_scores, key_block, preferred_element_type=jnp.float32
            )
            grad_key = jnp.einsum(
                "qhk,qhd->khd", grad_scores, queries, preferred_element_type=jnp.float32
            )
            grad_value = jnp.einsum(
                "qhk,qhd->khd", prob_low, grad_attended_low, preferred_element_type=jnp.float32
            )
            return (grad_query, (grad_key, grad_value))

        def skip_block(grad_query):
            empty_block = jnp.zeros((block_size, head_count, HD), jnp.float32)
            return (grad_query, (empty_block, empty_block))

        return lax.cond(key_first <= last_query, compute_block, skip_block, grad_query)

    grad_query, (key_grad_blocks, value_grad_blocks) = lax.scan(
        visit_back, zeros_rows, (key_blocks, value_blocks, seg_blocks, block_starts)
    )
    grad_keys, grad_values = (
        lax.psum_scatter(
            key_grad_blocks.reshape(total_rows, -1).astype(jnp.bfloat16),
            "ctx",
            scatter_dimension=0,
            tiled=True,
        ).astype(jnp.float32),
        lax.psum_scatter(
            value_grad_blocks.reshape(total_rows, -1).astype(jnp.bfloat16),
            "ctx",
            scatter_dimension=0,
            tiled=True,
        ).astype(jnp.float32),
    )
    grad_query = grad_query * softmax_scale
    grad_keys = grad_keys.reshape(local_rows, head_count, HD) * softmax_scale
    grad_query_back = rotate(grad_query, cosine_table, -sine_table).reshape(local_rows, -1)
    grad_keys_back = rotate(grad_keys, cosine_table, -sine_table).reshape(local_rows, -1)
    grad_projected = jnp.stack([grad_query_back, grad_keys_back, grad_values], axis=1).astype(
        jnp.bfloat16
    )
    grad_w_qkv = jnp.einsum(
        "td,tcm->dcm", norm_one, grad_projected, preferred_element_type=jnp.float32
    )
    grad_b_qkv = jnp.sum(grad_projected.astype(jnp.float32), axis=0)
    grad_norm_one = jnp.einsum(
        "tcm,dcm->td", grad_projected, qkv_all, preferred_element_type=jnp.float32
    )
    pull_one = jax.vjp(layer_norm, tokens, gain_one, bias_one)[1]
    input_one, grad_gain_one, grad_bias_one = pull_one(grad_norm_one)
    pull_two = jax.vjp(layer_norm, tokens, gain_two, bias_two)[1]
    input_two, grad_gain_two, grad_bias_two = pull_two(grad_norm_two)
    input_share = lax.psum_scatter(
        (input_one + input_two).astype(jnp.bfloat16), "tp", scatter_dimension=1, tiled=True
    ).astype(jnp.float32)
    grad_inputs = lax.dynamic_slice_in_dim(grad_float, share_start, share_width, 1) + input_share
    matrix_grads = (
        lax.psum_scatter(grad_w_qkv, ("dp", "ctx"), scatter_dimension=0, tiled=True),
        lax.psum_scatter(grad_w_out, ("dp", "ctx"), scatter_dimension=0, tiled=True),
        lax.psum_scatter(grad_w_up, ("dp", "ctx"), scatter_dimension=0, tiled=True),
        lax.psum_scatter(grad_w_down, ("dp", "ctx"), scatter_dimension=0, tiled=True),
    )
    vector_grads = lax.psum((grad_bias, grad_b_qkv, grad_b_up), ("dp", "ctx"))
    norm_totals = lax.psum(
        (grad_gain_one, grad_bias_one, grad_gain_two, grad_bias_two), ("dp", "ctx", "tp")
    )
    return (
        output[None],
        grad_inputs[None],
        norm_totals[0],
        norm_totals[1],
        norm_totals[2],
        norm_totals[3],
        matrix_grads[0],
        vector_grads[1],
        matrix_grads[1],
        vector_grads[0],
        matrix_grads[2],
        vector_grads[2],
        matrix_grads[3],
    )


def solution(mesh):
    return jax.shard_map(
        on_device,
        mesh=mesh,
        in_specs=(
            P("dp", "ctx", None),
            P("dp", "ctx"),
            P(),
            P(),
            P(),
            P(),
            P(("dp", "ctx"), None, "tp"),
            P(None, "tp"),
            P(("dp", "ctx"), "tp"),
            P(),
            P(("dp", "ctx"), "tp"),
            P("tp"),
            P(("dp", "ctx"), "tp"),
            P("dp", "ctx", None),
        ),
        out_specs=(
            P("dp", "ctx", "tp"),
            P("dp", "ctx", "tp"),
            P(),
            P(),
            P(),
            P(),
            P(("dp", "ctx"), None, "tp"),
            P(None, "tp"),
            P(("dp", "ctx"), "tp"),
            P(),
            P(("dp", "ctx"), "tp"),
            P("tp"),
            P(("dp", "ctx"), "tp"),
        ),
        check_vma=False,
    )
```

profile of v0, /device:TPU:0, one launch (start us, length us, event | category | flops | bytes accessed | tf_op | source)
XLA Modules:
  0.0 918.8 jit_solution(8912757698097167811)
XLA Ops:
  9.5 47.0 %all_gather.28 = bf16[768,384]{1,0:T(8,128)(2,1)S(1)} all-gather(bf16[48,384]{1,0:T(8,128)(2,1)} %param.30), channel_id=1, replica_groups=mesh['dp'=2,'ctx'=8,'tp'=2] {'dp','ctx'}, dimensions={0}, use_global_device_ids=true | all-gather | bytes 626688 | tf_op jit(solution)/shard_map/all_gather | solution.py:92
  56.5 1.2 convolution_convert_fusion
  57.9 16.2 %all-gather = bf16[1,1024]{1,0:T(2,128)(2,1)S(1)} all-gather(bf16[1,128]{1,0:T(2,128)(2,1)S(1)} %get-tuple-element.572), channel_id=2, replica_groups=mesh['dp'=2,'ctx'=8,'tp'=2] {'ctx'}, dimensions={1}, use_global_device_ids=true | all-gather | bytes 2304 | tf_op jit(solution)/shard_map/all_gather | solution.py:121
  76.1 0.7 fusion.54
  76.8 2.0 convolution_add_fusion.1
  79.8 31.3 %all_gather.26 = bf16[1024,384]{0,1:T(8,128)(2,1)S(1)} all-gather(bf16[128,384]{0,1:T(8,128)(2,1)S(1)} %bitcast.220), channel_id=1, replica_groups=mesh['dp'=2,'ctx'=8,'tp'=2] {'ctx'}, dimensions={0}, use_global_device_ids=true | all-gather | bytes 884736 | tf_op jit(solution)/shard_map/all_gather | solution.py:119
  111.6 33.1 %all-gather.1 = bf16[1024,1,384]{2,0,1:T(8,128)(2,1)S(1)} all-gather(bf16[128,1,384]{2,0,1:T(8,128)(2,1)S(1)} %slice.101), channel_id=3, replica_groups=mesh['dp'=2,'ctx'=8,'tp'=2] {'ctx'}, dimensions={0}, use_global_device_ids=true | all-gather | bytes 884736 | tf_op jit(solution)/shard_map/all_gather | solution.py:120
  145.6 1.0 copy.78
  146.8 19.0 %conditional.2 = (f32[128,6]{0,1:T(8,128)}, f32[128,6]{0,1:T(8,128)}, f32[128,6,64]{0,2,1:T(8,128)}, f32[128,6]{0,1:T(8,128)S(1)}) conditional(s32[]{:T(128)} %convert_element_type.120, () %tuple.42, (s32[2]{0:T(128)}, s32[128]{0:T(128)}, bf16[2,512]{1,0:T(2,128)(2,1)S(1)}, bf16[128]{0:T(256)(128)(2,1)S(1)}, bf16[2,512,6,64]{1,0,3,2:T(2,128)(2,1)S(1)}, ...), branch_computations={%region_2.0_spmd, %region_3.8_spmd} | conditional | flops 104681728 | bytes 12615769 | solution.py:152
  146.8 1.1 copy.75
  147.9 1.0 copy.76
  148.8 16.2 %while.32 = (s32[]{:T(128)}, f32[128,6]{0,1:T(8,128)}, f32[128,6]{0,1:T(8,128)}, f32[128,6,64]{0,2,1:T(8,128)}, s32[2]{0:T(128)}, /*index=5*/s32[128]{0:T(128)},...) while((s32[]{:T(128)}, f32[128,6]{0,1:T(8,128)}, ...), condition=%wide.region_7.7_spmd.clone, body=%wide.region_4.6_spmd.clone.sunk | while | flops 104681728 | bytes 9463753 | solution.py:150
  148.8 1.2 dynamic_slice.97
  150.8 0.9 compare_and_fusion.3
  151.6 1.5 fusion.100
  154.6 1.1 fusion.103
  155.7 1.2 dynamic_slice.97
  157.7 0.9 compare_and_fusion.3
  158.5 1.5 fusion.100
  160.0 0.8 select_maximum_fusion.2
  161.1 1.3 fusion.102
  163.0 2.0 fusion.103
  166.4 1.0 multiply_reduce_fusion.5
  167.4 10.7 %while.33 = (s32[]{:T(128)}, f32[128,6,64]{0,2,1:T(8,128)S(1)}, bf16[2,512,6,64]{1,3,2,0:T(8,128)(2,1)}, bf16[2,512,6,64]{1,3,2,0:T(8,128)(2,1)}, s32[2]{0:T(128...) while((s32[]{:T(128)}, f32[128,6,64]{0,2,1:T(8,128)S(1)}, ...), condition=%wide.region_13.14_spmd.clone, body=%wide.region_10.13_spmd.clone.sunk | while | flops 254788224 | bytes 14698087 | solution.py:233
  167.4 1.2 dynamic_slice.93
  169.3 4.8 conditional.5
  170.3 1.5 fusion.5
  172.3 0.8 copy-done.1
  174.1 1.0 constant_dynamic-update-slice_fusion.3
  175.1 1.2 dynamic_slice.93
  177.1 1.0 constant_dynamic-update-slice_fusion.3
  178.2 1.9 copy.80
  180.2 1.2 copy.96
  181.5 1.9 copy.81
  183.6 1.2 copy.82
  185.7 1.1 fusion.67
  186.8 5.0 multiply_convert_fusion
  191.8 17.7 %all-gather.10.cloned.1.call-done = bf16[768,1536]{1,0:T(8,128)(2,1)} async-done(((bf16[48,1536]{1,0:T(8,128)(2,1)}), bf16[768,1536]{1,0:T(8,128)(2,1)}) %all-gather.10.cloned.1.call-update) | async-done | bytes 2359312 | tf_op jit(solution)/shard_map/all_gather | solution.py:94
  209.5 3.4 fusion.35
  212.9 1.7 copy.94
  214.7 2.8 convert_reduce_fusion
  217.5 0.9 fusion.68
  218.4 55.5 %reduce-scatter.27.cloned.1.call-done = bf16[128,384]{1,0:T(8,128)(2,1)} async-done(((bf16[1024,384]{1,0:T(8,128)(2,1)}), bf16[128,384]{1,0:T(8,128)(2,1)}) %reduce-scatter.27.cloned.1.call-update) | async-done | bytes 98320
  273.9 1.6 copy.97
  275.5 0.9 convert_multiply_fusion
  276.5 0.8 subtract_convert_fusion.1
  277.2 1.6 pad_maximum_fusion.3
  278.9 1.0 copy.83
  279.9 58.9 %reduce-scatter.19.cloned.1.call-done = bf16[128,384]{1,0:T(8,128)(2,1)} async-done(((bf16[1024,384]{1,0:T(8,128)(2,1)}), bf16[128,384]{1,0:T(8,128)(2,1)}) %reduce-scatter.19.cloned.1.call-update) | async-done | bytes 98320 | tf_op jit(solution)/shard_map/reduce_scatter | solution.py:243
  338.9 2.2 fusion.64
  341.9 0.8 copy.98
  343.1 1.4 copy.100
  344.7 2.5 fusion.57
  347.9 3.0 fusion.60
  350.9 3.0 convolution_bitcast_fusion.4
  354.0 6.1 copy.102
  361.0 1.0 copy.95
  362.7 40.3 %all-reduce = (f32[768]{0:T(1024)}, f32[768]{0:T(1024)}, f32[768]{0:T(1024)}, f32[768]{0:T(1024)}) all-reduce(f32[768]{0:T(1024)S(1)} %get-tuple-element.480, f32[768]{0:T(1024)S(1)} %copy-done.23, f32[768]{0:T(1024)S(1)} %get-tuple-element.471, f32[768]{0:T(1024)S(1)} %copy-done.24), channel_id=1, replica_groups=mesh['dp'=2,'ctx'=8,'tp'=2] {'dp','ctx','tp'}, use_global_device_ids=true, to_apply=%region_22.23 | all-reduce | flops 3072 | bytes 24576 | tf_op jit(solution)/shard_map/psum | solution.py:279
  403.1 75.9 %all-reduce.1 = (f32[3,384]{1,0:T(4,128)}, f32[768]{0:T(1024)}, f32[1536]{0:T(1024)}) all-reduce(f32[3,384]{1,0:T(4,128)S(1)} %convert_reduce_fusion.1, f32[768]{0:T(1024)S(1)} %fusion.52, f32[1536]{0:T(1024)S(1)} %copy-done.21), channel_id=1, replica_groups=mesh['dp'=2,'ctx'=8,'tp'=2] {'dp','ctx'}, use_global_device_ids=true, to_apply=%region_31.32 | all-reduce | flops 3456 | bytes 27648 | tf_op jit(solution)/shard_map/psum | solution.py:278
  479.0 1.0 copy.99
  480.7 9.2 %reduce-scatter.31.cloned.1.call-done = f32[48,384]{1,0:T(8,128)} async-done(((f32[768,384]{1,0:T(8,128)}), f32[48,384]{1,0:T(8,128)}) %reduce-scatter.31.cloned.1.call-update) | async-done | bytes 73744
  489.9 138.2 %reduce-scatter.21.cloned.1.call-done = f32[48,3,384]{2,0,1:T(8,128)} async-done(((f32[768,3,384]{2,0,1:T(8,128)}), f32[48,3,384]{2,0,1:T(8,128)}) %reduce-scatter.21.cloned.1.call-update) | async-done | bytes 221200 | tf_op jit(solution)/shard_map/reduce_scatter | solution.py:273
  628.1 141.3 %reduce-scatter.23.cloned.1.call-done = f32[48,1536]{1,0:T(8,128)} async-done(((f32[768,1536]{1,0:T(8,128)}), f32[48,1536]{1,0:T(8,128)}) %reduce-scatter.23.cloned.1.call-update) | async-done | bytes 294928 | tf_op jit(solution)/shard_map/reduce_scatter | solution.py:275
  769.5 142.8 %reduce-scatter.33.cloned.1.call-done = f32[48,1536]{1,0:T(8,128)} async-done(((f32[768,1536]{1,0:T(8,128)}), f32[48,1536]{1,0:T(8,128)}) %reduce-scatter.33.cloned.1.call-update) | async-done | bytes 294928
  (167 shorter events, 20.2 us)
Async XLA Ops:
  7.2 50.7 %copy-start.31 = (s32[1,128]{1,0:T(1,128)S(1)}, s32[1,128]{1,0:T(1,128)}, u32[]{:S(2)}) copy-start(s32[1,128]{1,0:T(1,128)} %param.23) | copy-start | bytes 1540
  7.2 68.0 %copy-start = (bf16[1,128,768]{2,1,0:T(8,128)(2,1)S(1)}, bf16[1,128,768]{2,1,0:T(8,128)(2,1)}, u32[]{:S(2)}) copy-start(bf16[1,128,768]{2,1,0:T(8,128)(2,1)} %param.22) | copy-start | bytes 589828
  7.2 69.6 %copy-start.22 = (f32[3,384]{1,0:T(4,128)S(1)}, f32[3,384]{1,0:T(4,128)}, u32[]{:S(2)}) copy-start(f32[3,384]{1,0:T(4,128)} %param.29) | copy-start | bytes 13828
  7.2 69.6 %copy-start.15 = (f32[768]{0:T(1024)S(1)}, f32[768]{0:T(1024)}, u32[]{:S(2)}) copy-start(f32[768]{0:T(1024)} %param.25) | copy-start | bytes 9220
  7.2 69.6 %copy-start.13 = (f32[768]{0:T(1024)S(1)}, f32[768]{0:T(1024)}, u32[]{:S(2)}) copy-start(f32[768]{0:T(1024)} %param.24) | copy-start | bytes 9220
  7.2 69.5 %all-gather.6.cloned.1.call-start = ((), (), s32[]{:S(2)}) async-start(), calls=%async_computation.8 | async-start | bytes 1880064 | tf_op jit(solution)/shard_map/all_gather | solution.py:91
  8.0 178.8 %all-gather.8.cloned.1.call-start = ((), (), s32[]{:S(2)}) async-start(), calls=%async_computation.9 | async-start | bytes 2506752 | tf_op jit(solution)/shard_map/all_gather | solution.py:93
  8.7 200.8 %all-gather.10.cloned.1.call-start = ((), (), s32[]{:S(2)}) async-start(), calls=%async_computation.10 | async-start | bytes 2506752 | tf_op jit(solution)/shard_map/all_gather | solution.py:94
  9.4 264.4 %reduce-scatter.27.cloned.1.call-start = ((), (), s32[]{:S(2)}) async-start(), calls=%async_computation.15 | async-start | bytes 884736
  75.5 0.6 copy-start.27
  76.1 2.8 copy-start.17
  145.6 1.1 copy-start.12
  153.1 1.5 copy-start.2
  160.0 3.0 copy-start.2
  167.4 18.3 %copy-start.8 = (bf16[128,6,64]{0,2,1:T(8,128)(2,1)}, bf16[128,6,64]{0,2,1:T(8,128)(2,1)S(1)}, u32[]{:S(2)}) copy-start(bf16[128,6,64]{0,2,1:T(8,128)(2,1)S(1)} %get-tuple-element.561) | copy-start | bytes 294916
  171.8 1.3 copy-start.1
  181.4 157.4 %reduce-scatter.19.cloned.1.call-start = ((), (), s32[]{:S(2)}) async-start(), calls=%async_computation.11 | async-start | bytes 884736 | tf_op jit(solution)/shard_map/reduce_scatter | solution.py:243
  184.7 2.1 copy-start.14
  184.7 2.1 copy-start.18
  184.7 2.1 copy-start.25
  184.7 2.1 copy-start.30
  184.8 176.2 %reduce-scatter.25.cloned.1.call-start = ((), (), s32[]{:S(2)}) async-start(), calls=%async_computation.14 | async-start | bytes 294912
  185.0 6.8 copy-start.10
  186.8 22.7 %copy-start.7 = (f32[128,768]{1,0:T(8,128)S(1)}, f32[128,768]{1,0:T(8,128)}, u32[]{:S(2)}) copy-start(f32[128,768]{1,0:T(8,128)} %fusion.67) | copy-start | bytes 1179652
  209.5 5.2 copy-start.3
  209.5 5.2 copy-start.4
  214.6 264.3 %reduce-scatter.29.cloned.1.call-start = ((), (), s32[]{:S(2)}) async-start(), calls=%async_computation.16 | async-start | bytes 294912
  214.7 2.8 copy-start.5
  217.5 121.4 %copy-start.6 = (bf16[768,3,384]{2,0,1:T(8,128)(2,1)S(1)}, bf16[768,3,384]{2,0,1:T(8,128)(2,1)}, u32[]{:S(2)}) copy-start(bf16[768,3,384]{2,0,1:T(8,128)(2,1)} %all-gather.6.cloned.1.call-done) | copy-start | bytes 5308420
  338.9 2.2 copy-start.28
  338.9 2.3 copy-start.19
  341.1 1.7 copy-start.9
  342.7 147.2 %reduce-scatter.31.cloned.1.call-start = ((), (), s32[]{:S(2)}) async-start(), calls=%async_computation.17 | async-start | bytes 1253376
  343.1 1.5 copy-start.11
  343.1 1.5 copy-start.16
  343.1 1.5 copy-start.20
  344.6 283.5 %reduce-scatter.21.cloned.1.call-start = ((), (), s32[]{:S(2)}) async-start(), calls=%async_computation.12 | async-start | bytes 3760128 | tf_op jit(solution)/shard_map/reduce_scatter | solution.py:273
  347.2 0.7 copy-start.26
  347.2 422.3 %reduce-scatter.23.cloned.1.call-start = ((), (), s32[]{:S(2)}) async-start(), calls=%async_computation.13 | async-start | bytes 5013504 | tf_op jit(solution)/shard_map/reduce_scatter | solution.py:275
  350.9 561.4 %reduce-scatter.33.cloned.1.call-start = ((), (), s32[]{:S(2)}) async-start(), calls=%async_computation.18 | async-start | bytes 5013504
  360.1 0.7 copy-start.29
  360.1 2.6 copy-start.23
  360.2 2.6 copy-start.24
  360.2 42.9 %copy-start.21 = (f32[1536]{0:T(1024)S(1)}, f32[1536]{0:T(1024)}, u32[]{:S(2)}) copy-start(f32[1536]{0:T(1024)} %get-tuple-element.575) | copy-start | bytes 18436
Sparse Core Ops, SparseCore 0:
  10.9 62.9 all-gather.5
  76.7 68.6 all-gather.7
  148.1 61.3 all-gather.9
  212.7 61.1 reduce-scatter.26
  277.4 61.4 reduce-scatter.18
  341.5 6.5 reduce-scatter.24
  350.9 8.7 reduce-scatter.28
  365.0 124.8 reduce-scatter.30
  495.6 132.5 reduce-scatter.20
  633.7 135.7 reduce-scatter.22
  776.1 136.1 reduce-scatter.32
where the time goes:
time: 920 us; the launch traced here: 919 us
  waiting for transfers between devices  566 us (62%)
  blocking collectives  244 us (27%)
  local copies, waits for them, and re-layouts  39.5 us (4%)
  matrix products  36.4 us (4%)
  other arithmetic  16.5 us (2%)
  between operations  14.5 us (2%)
    unnamed x16, waiting for transfers between devices  210 us
    reduce_scatter x1, waiting for transfers between devices, on_device(): lax.psum_scatter(grad_w_up, ('dp', 'ctx'), scatter_dimension=0, tiled=True)  141 us
    reduce_scatter x1, waiting for transfers between devices, on_device(): lax.psum_scatter(grad_w_qkv, ('dp', 'ctx'), scatter_dimension=0, tiled=True)  138 us
    psum x1, blocking collectives, on_device(): vector_grads = lax.psum((grad_bias, grad_b_qkv, grad_b_up), ('dp', 'ctx'))  75.9 us
    reduce_scatter x1, waiting for transfers between devices, on_device(): lax.psum_scatter(value_grad_blocks.reshape(total_rows, -1).astype(jnp.bfl...  58.9 us
    all_gather x1, blocking collectives, on_device(): lax.all_gather(w_out, ('dp', 'ctx'), axis=0, tiled=True)  47 us
    psum x1, blocking collectives, on_device(): lax.psum((grad_gain_one, grad_bias_one, grad_gain_two, grad_bias_two), ('...  40.3 us
    all_gather x1, blocking collectives, on_device(): value_piece = lax.all_gather(value_flat, 'ctx', axis=0, tiled=True)  33.1 us
  transfers between devices with their start and end apart: 11, of which 7 were waited for; matrix products, arithmetic and copies ran while one was open for 10% of the time, Pallas kernels for 0%

commit v1 on v0

v1 whole, which is shorter than its diff:
```python
import math

import jax
import jax.numpy as jnp
from jax import lax
from jax.sharding import PartitionSpec as P

HD = 64
ROT = 16

NORM_EPSILON = 1e-05
NEG_LARGE = -1e30
LAST = (((1,), (1,)), ((), ()))
ROWS = (((0,), (0,)), ((), ()))


def dot_f32(a, b, dims=(((1,), (0,)), ((), ()))):
    return lax.dot_general(a, b, dims, preferred_element_type=jnp.float32)


def angle_tables(first_row, length):
    positions = (first_row + jnp.arange(length)).astype(jnp.float32)
    frequency = 10000.0 ** (-(jnp.arange(ROT // 2).astype(jnp.float32) * 2.0 / ROT))
    angles = positions[:, None] * frequency[None, :]
    return (jnp.cos(angles), jnp.sin(angles))


def rotate(values, cosine_table, sine_table):
    half_rot = ROT // 2
    lower = values[..., :half_rot]
    upper = values[..., half_rot : 2 * half_rot]
    return jnp.concatenate(
        [
            lower * cosine_table - upper * sine_table,
            upper * cosine_table + lower * sine_table,
            values[..., 2 * half_rot :],
        ],
        axis=-1,
    )


def gather_tokens(packed):
    return lax.all_gather(packed, "ctx", axis=0, tiled=True)


def weights_to_columns(blocks):
    received = lax.all_to_all(blocks, "ctx", 0, 0, tiled=True)
    return lax.all_gather(received, "dp", axis=0, tiled=False)


def grads_to_owners(blocks):
    dp, ctx = blocks.shape[:2]
    mine = lax.psum_scatter(blocks, "dp", scatter_dimension=0, tiled=False)
    return lax.all_to_all(mine, "ctx", 0, 0, tiled=True)


def scatter_sum(partial, ctx, tp):
    rows, width = partial.shape
    parts = partial.reshape(ctx, rows // ctx, tp, width // tp).transpose(0, 2, 1, 3)
    parts = parts.reshape(ctx * tp, rows // ctx, width // tp)
    return lax.psum_scatter(parts, ("ctx", "tp"), scatter_dimension=0, tiled=False)


def on_device(
    inputs,
    segments,
    gain_one,
    bias_one,
    gain_two,
    bias_two,
    w_qkv,
    b_qkv,
    w_out,
    out_bias,
    w_up,
    b_up,
    w_down,
    cotangent,
):
    f32, bf16 = jnp.float32, jnp.bfloat16
    dp, ctx, tp = lax.axis_size("dp"), lax.axis_size("ctx"), lax.axis_size("tp")
    my_ctx, my_tp = lax.axis_index("ctx"), lax.axis_index("tp")
    local_rows, width = inputs.shape[1:]
    length = local_rows * ctx
    share = width // tp
    owned = w_qkv.shape[0]
    heads = w_qkv.shape[2] // HD
    slots = -(-heads // ctx)
    head_width = slots * HD
    units = w_up.shape[1] // ctx
    pad_heads = slots * ctx * HD - heads * HD

    qkv_blocks = jnp.pad(w_qkv, ((0, 0), (0, 0), (0, pad_heads)))
    qkv_blocks = qkv_blocks.reshape(owned, 3, ctx, head_width).transpose(2, 0, 1, 3)
    out_blocks = jnp.pad(w_out, ((0, 0), (0, pad_heads))).reshape(owned, ctx, head_width)
    blocks = jnp.concatenate(
        [
            w_up.reshape(owned, ctx, units).transpose(1, 0, 2),
            w_down.reshape(owned, ctx, units).transpose(1, 0, 2),
            qkv_blocks.reshape(ctx, owned, 3 * head_width),
            out_blocks.transpose(1, 0, 2),
        ],
        axis=-1,
    )
    columns = weights_to_columns(blocks).reshape(width, -1)
    up = columns[:, :units]
    down = columns[:, units : 2 * units]
    qkv = columns[:, 2 * units : 2 * units + 3 * head_width]
    out = columns[:, 2 * units + 3 * head_width :]

    seg_columns = jnp.broadcast_to(segments[0].astype(bf16)[:, None], (local_rows, 128))
    packed = jnp.concatenate([inputs[0], cotangent[0], seg_columns], axis=-1)
    row = gather_tokens(packed)
    tokens = row[:, :width].astype(f32)
    grad_out = row[:, width : 2 * width]
    seg = row[:, 2 * width]

    qkv_bias = jnp.pad(b_qkv, ((0, 0), (0, pad_heads))).reshape(3, ctx, head_width)
    qkv_bias = lax.dynamic_index_in_dim(qkv_bias, my_ctx, 1, keepdims=False).reshape(-1)
    up_bias = lax.dynamic_slice_in_dim(b_up, my_ctx * units, units, 0)

    average = jnp.mean(tokens, axis=-1, keepdims=True)
    centered = tokens - average
    inverse = lax.rsqrt(jnp.mean(centered * centered, axis=-1, keepdims=True) + NORM_EPSILON)
    xhat = centered * inverse
    norm_one = (xhat * gain_one + bias_one).astype(bf16)
    norm_two = (xhat * gain_two + bias_two).astype(bf16)

    projected = dot_f32(norm_one, qkv) + qkv_bias
    cosine_table, sine_table = angle_tables(0, length)
    softmax_scale = 1.0 / math.sqrt(HD)
    position = jnp.arange(length)
    allowed = (position[None, :] <= position[:, None]) & (seg[None, :] == seg[:, None])
    kept = []
    for slot in range(slots):
        first = slot * HD
        query = rotate(projected[:, first : first + HD], cosine_table, sine_table).astype(bf16)
        first += head_width
        key = rotate(projected[:, first : first + HD], cosine_table, sine_table).astype(bf16)
        first += head_width
        value = projected[:, first : first + HD].astype(bf16)
        scores = jnp.where(allowed, dot_f32(query, key, LAST) * softmax_scale, NEG_LARGE)
        exponent = jnp.exp(scores - jnp.max(scores, axis=-1, keepdims=True))
        softmax = exponent / jnp.sum(exponent, axis=-1, keepdims=True)
        attended = dot_f32(softmax.astype(bf16), value)
        kept.append((query, key, value, softmax, attended))
    attended_low = jnp.concatenate([item[4] for item in kept], axis=-1).astype(bf16)

    pre_gelu = dot_f32(norm_two, up) + up_bias
    activated = jax.nn.gelu(pre_gelu, approximate=False).astype(bf16)
    branch = dot_f32(attended_low, out, LAST) + dot_f32(activated, down, LAST)
    branch_share = scatter_sum(branch.astype(bf16), ctx, tp).astype(f32)

    grad_attended = dot_f32(grad_out, out).astype(bf16)
    grad_activated = dot_f32(grad_out, down)
    gelu_pull = jax.vjp(lambda current: jax.nn.gelu(current, approximate=False), pre_gelu)[1]
    grad_pre = gelu_pull(grad_activated)[0].astype(bf16)
    grad_w_out = dot_f32(grad_out, attended_low, ROWS)
    grad_w_down = dot_f32(grad_out, activated, ROWS)
    grad_w_up = dot_f32(norm_two, grad_pre, ROWS)
    grad_b_up = jnp.sum(grad_pre.astype(f32), axis=0)
    grad_norm_two = dot_f32(grad_pre, up, LAST)

    pieces = ([], [], [])
    for slot, (query, key, value, softmax, attended) in enumerate(kept):
        grad_rows = grad_attended[:, slot * HD : (slot + 1) * HD]
        grad_dots = jnp.sum(grad_rows.astype(f32) * attended, axis=-1, keepdims=True)
        grad_probs = dot_f32(grad_rows, value, LAST)
        grad_scores = (softmax * (grad_probs - grad_dots)).astype(bf16)
        grad_query = dot_f32(grad_scores, key) * softmax_scale
        grad_key = dot_f32(grad_scores, query, ROWS) * softmax_scale
        pieces[0].append(rotate(grad_query, cosine_table, -sine_table))
        pieces[1].append(rotate(grad_key, cosine_table, -sine_table))
        pieces[2].append(dot_f32(softmax.astype(bf16), grad_rows, ROWS))
    grad_projected = jnp.concatenate(pieces[0] + pieces[1] + pieces[2], axis=-1).astype(bf16)
    grad_w_qkv = dot_f32(norm_one, grad_projected, ROWS)
    grad_b_qkv = jnp.sum(grad_projected.astype(f32), axis=0)
    grad_norm_one = dot_f32(grad_projected, qkv, LAST)

    grad_gain_one = jnp.sum(grad_norm_one * xhat, axis=0)
    grad_bias_one = jnp.sum(grad_norm_one, axis=0)
    grad_gain_two = jnp.sum(grad_norm_two * xhat, axis=0)
    grad_bias_two = jnp.sum(grad_norm_two, axis=0)
    pulled = grad_norm_one * gain_one + grad_norm_two * gain_two
    input_term = inverse * (
        pulled
        - jnp.mean(pulled, axis=-1, keepdims=True)
        - xhat * jnp.mean(pulled * xhat, axis=-1, keepdims=True)
    )
    input_share = scatter_sum(input_term.astype(bf16), ctx, tp).astype(f32)

    grads = jnp.concatenate([grad_w_up, grad_w_down, grad_w_qkv, grad_w_out], axis=-1)
    grads = grads.astype(bf16).reshape(dp, ctx, owned, -1)
    own = grads_to_owners(grads).astype(f32)
    own_up = own[:, :, :units].transpose(1, 0, 2).reshape(owned, -1)
    own_down = own[:, :, units : 2 * units].transpose(1, 0, 2).reshape(owned, -1)
    own_qkv = own[:, :, 2 * units : 2 * units + 3 * head_width]
    own_qkv = own_qkv.reshape(ctx, owned, 3, head_width).transpose(1, 2, 0, 3)
    own_qkv = own_qkv.reshape(owned, 3, ctx * head_width)[:, :, : heads * HD]
    own_out = own[:, :, 2 * units + 3 * head_width :].transpose(1, 0, 2)
    own_out = own_out.reshape(owned, -1)[:, : heads * HD]

    grad_bias = jnp.sum(cotangent[0].astype(f32), axis=0) * (my_tp == 0).astype(f32)
    place = (jnp.arange(tp)[:, None] == my_tp) & (jnp.arange(ctx)[None, :] == my_ctx)
    local = jnp.concatenate([grad_b_qkv, grad_b_up])
    spread = jnp.where(place[:, :, None], local, 0.0)
    total = lax.psum(
        jnp.concatenate(
            [
                grad_gain_one,
                grad_bias_one,
                grad_gain_two,
                grad_bias_two,
                grad_bias,
                spread.reshape(-1),
            ]
        ),
        ("dp", "ctx", "tp"),
    )
    spread = total[5 * width :].reshape(tp, ctx, -1)
    spread = lax.dynamic_index_in_dim(spread, my_tp, 0, keepdims=False)
    sum_b_qkv = spread[:, : 3 * head_width].reshape(ctx, 3, head_width).transpose(1, 0, 2)
    sum_b_qkv = sum_b_qkv.reshape(3, -1)[:, : heads * HD]
    sum_b_up = spread[:, 3 * head_width :].reshape(-1)

    start = my_tp * share
    token_share = lax.dynamic_slice_in_dim(inputs[0], start, share, 1).astype(f32)
    bias_share = lax.dynamic_slice_in_dim(out_bias, start, share, 0)
    cotangent_share = lax.dynamic_slice_in_dim(cotangent[0], start, share, 1).astype(f32)
    output = token_share + branch_share + bias_share
    grad_inputs = cotangent_share + input_share
    return (
        output[None],
        grad_inputs[None],
        total[:width],
        total[width : 2 * width],
        total[2 * width : 3 * width],
        total[3 * width : 4 * width],
        own_qkv,
        sum_b_qkv,
        own_out,
        total[4 * width : 5 * width],
        own_up,
        sum_b_up,
        own_down,
    )


def solution(mesh):
    return jax.shard_map(
        on_device,
        mesh=mesh,
        in_specs=(
            P("dp", "ctx", None),
            P("dp", "ctx"),
            P(),
            P(),
            P(),
            P(),
            P(("dp", "ctx"), None, "tp"),
            P(None, "tp"),
            P(("dp", "ctx"), "tp"),
            P(),
            P(("dp", "ctx"), "tp"),
            P("tp"),
            P(("dp", "ctx"), "tp"),
            P("dp", "ctx", None),
        ),
        out_specs=(
            P("dp", "ctx", "tp"),
            P("dp", "ctx", "tp"),
            P(),
            P(),
            P(),
            P(),
            P(("dp", "ctx"), None, "tp"),
            P(None, "tp"),
            P(("dp", "ctx"), "tp"),
            P(),
            P(("dp", "ctx"), "tp"),
            P("tp"),
            P(("dp", "ctx"), "tp"),
        ),
        check_vma=False,
    )
```

time: 920 us -> 285 us (0.31)
  waiting for transfers between devices: 566 us -> 133 us
  blocking collectives: 244 us -> 49 us
  local copies, waits for them, and re-layouts: 39.5 us -> 27.5 us
  starting transfers between devices: 0.62 us -> 12.5 us
    reduce_scatter x3, waiting for transfers between devices: 339 us -> 78.8 us  [the longest x2 78.8 us: scatter_sum(): lax.psum_scatter(parts, ('ctx', 'tp'), scatter_dimension=0, tiled=False)]
    unnamed x16 -> x4, waiting for transfers between devices: 210 us -> 0.07 us
    all_gather x4 -> x1, blocking collectives: 128 us -> 9.6 us  [weights_to_columns(): return lax.all_gather(received, 'dp', axis=0, tiled=False)]
    psum x2 -> x1, blocking collectives: 116 us -> 39.4 us  [on_device(): lax.psum(jnp.concatenate([grad_gain_one, grad_bias_one, grad_gain_two, gr...]
    all_to_all x0 -> x2, waiting for transfers between devices: none -> 24 us  [the longest x1 24 us: weights_to_columns(): received = lax.all_to_all(blocks, 'ctx', 0, 0, tiled=True)]
    unnamed x72 -> x58, local copies, waits for them, and re-layouts: 18.2 us -> 1.7 us
    all_gather x3 -> x1, waiting for transfers between devices: 17.7 us -> 30.2 us  [gather_tokens(): return lax.all_gather(packed, 'ctx', axis=0, tiled=True)]
    all_to_all x0 -> x2, starting transfers between devices: none -> 12.3 us  [the longest x1 7.25 us: weights_to_columns(): received = lax.all_to_all(blocks, 'ctx', 0, 0, tiled=True)]
  transfers between devices with their start and end apart: 11 -> 6, of which waited for: 7 -> 4; matrix products, arithmetic and copies ran while one was open for 10% -> 10% of each run, Pallas kernels for 0% -> 0%
where the time goes in v1:
time: 285 us; the launch traced here: 284 us
  waiting for transfers between devices  133 us (47%)
  blocking collectives  49 us (17%)
  matrix products  30.7 us (11%)
  local copies, waits for them, and re-layouts  27.5 us (10%)
  other arithmetic  17.2 us (6%)
  between operations  14.4 us (5%)
  starting transfers between devices  12.5 us (4%)
    reduce_scatter x2, waiting for transfers between devices, scatter_sum(): lax.psum_scatter(parts, ('ctx', 'tp'), scatter_dimension=0, tiled=False)  78.8 us
    psum x1, blocking collectives, on_device(): lax.psum(jnp.concatenate([grad_gain_one, grad_bias_one, grad_gain_two, gr...  39.4 us
    dot_general x18, matrix products, dot_f32(): return lax.dot_general(a, b, dims, preferred_element_type=jnp.float32)  30.7 us
    all_gather x1, waiting for transfers between devices, gather_tokens(): return lax.all_gather(packed, 'ctx', axis=0, tiled=True)  30.2 us
    all_to_all x1, waiting for transfers between devices, weights_to_columns(): received = lax.all_to_all(blocks, 'ctx', 0, 0, tiled=True)  24 us
    all_gather x1, blocking collectives, weights_to_columns(): return lax.all_gather(received, 'dp', axis=0, tiled=False)  9.6 us
    all_to_all x1, starting transfers between devices, weights_to_columns(): received = lax.all_to_all(blocks, 'ctx', 0, 0, tiled=True)  7.25 us
  transfers between devices with their start and end apart: 6, of which 4 were waited for; matrix products, arithmetic and copies ran while one was open for 10% of the time, Pallas kernels for 0%

profile of v1, /device:TPU:0, one launch (start us, length us, event | category | flops | bytes accessed | tf_op | source)
XLA Modules:
  0.0 284.4 jit_solution(16462466146605602740)
XLA Ops:
  7.3 0.7 convert_bitcast_fusion
  8.1 1.8 pad_maximum_fusion.2
  9.9 0.9 pad.12
  11.1 0.3 copy.106
  11.3 0.2 reshape.197
  12.4 0.9 copy.90
  13.3 7.3 %all-to-all-start = ((bf16[8,48,640]{2,1,0:T(8,128)(2,1)}), bf16[8,48,640]{2,1,0:T(8,128)(2,1)S(1)}, u32[]{:S(2)}, u32[]{:S(2)}) async-start(bf16[8,48,640]{2,1,0:T(8,128)(2,1)} %copy.90), calls=%async_computation | async-start | bytes 983040 | tf_op jit(solution)/shard_map/all_to_all | solution.py:47
  20.8 1.3 dynamic_slice.22
  22.1 24.0 %all-to-all-done = bf16[8,48,640]{2,1,0:T(8,128)(2,1)S(1)} async-done(((bf16[8,48,640]{2,1,0:T(8,128)(2,1)}), bf16[8,48,640]{2,1,0:T(8,128)(2,1)S(1)}, u32[]{:S(2)}, u32[]{:S(2)}) %all-to-all-start) | async-done | bytes 491552 | tf_op jit(solution)/shard_map/all_to_all | solution.py:47
  46.1 9.6 %all-gather = bf16[16,48,640]{2,1,0:T(8,128)(2,1)} all-gather(bf16[8,48,640]{2,1,0:T(8,128)(2,1)S(1)} %all-to-all-done), channel_id=2, replica_groups=mesh['dp'=2,'ctx'=8,'tp'=2] {'dp'}, dimensions={0}, use_global_device_ids=true | all-gather | bytes 1474560 | tf_op jit(solution)/shard_map/all_gather | solution.py:48
  55.7 30.2 %all-gather.3.cloned.1.call-done = bf16[1024,1664]{1,0:T(8,128)(2,1)} async-done(((bf16[128,1664]{1,0:T(8,128)(2,1)}), bf16[1024,1664]{1,0:T(8,128)(2,1)}) %all-gather.3.cloned.1.call-update) | async-done | bytes 3407888 | tf_op jit(solution)/shard_map/all_gather | solution.py:43
  86.0 1.8 convert_reduce_fusion
  87.7 2.0 fusion.21
  89.8 2.6 fusion.99
  92.4 0.2 fusion.81
  92.8 1.0 fusion.100
  93.8 0.6 fusion.10
  94.4 0.7 fusion.22
  95.1 0.7 convolution_convert_fusion.4
  95.8 0.5 multiply_reduce_fusion
  96.3 1.1 multiply_convert_fusion
  97.4 0.8 convolution_multiply_fusion.1
  98.1 0.5 convolution_multiply_fusion
  98.8 0.2 constant_dynamic-update-slice_fusion.2
  99.5 0.8 fusion.23
  100.3 0.8 copy-done.2
  101.1 1.6 convolution_convert_fusion
  102.7 1.9 copy.96
  104.6 4.4 %multiply_convert_fusion.1 = (bf16[1024,192]{0,1:T(8,128)(2,1)}, f32[1024,192]{0,1:T(8,128)S(1)}, f32[1024,192]{0,1:T(8,128)S(1)}) fusion(f32[192]{0:T(256)S(1)} %copy-done.15, bf16[768,640]{1,0:T(8,128)(2,1)} %bitcast.55, f32[768]{0:T(1024)S(1)} %copy-done.19, f32[768]{0:T(1024)} %param.18, f32[1024]{0:T(1024)S(1)} %add_rsqrt_fusion, ...), kind=kOutput, calls=%fused_computation.53 | convolution fusion | flops 319684608 | bytes 3949568 | tf_op jit(solution)/shard_map/dot_general | solution.py:18
  108.9 2.9 %convert_reduce_fusion.1 = (f32[192]{0:T(256)}, bf16[1024,192]{0,1:T(8,128)(2,1)S(1)}) fusion(f32[1024,192]{0,1:T(8,128)S(1)} %get-tuple-element.21, f32[1024,192]{0,1:T(8,128)S(1)} %get-tuple-element.41, bf16[768,640]{1,0:T(8,128)(2,1)} %bitcast.56, bf16[1024,1664]{1,0:T(8,128)(2,1)S(1)} %copy-done), kind=kOutput, calls=%fused_computation.50 | convolution fusion | flops 305135424 | bytes 3932928 | tf_op jit(solution)/shard_map/dot_general | solution.py:18
  111.8 0.8 copy-done.24
  112.6 1.6 convolution_convert_fusion.2
  114.2 1.9 copy.94
  116.1 1.0 convolution_convert_fusion.5
  117.1 1.7 copy.104
  118.8 2.2 convolution_convert_fusion.1
  121.0 1.9 copy.95
  122.9 2.7 pad_maximum_fusion
  125.7 1.8 fusion.42
  127.5 4.0 %fusion.20 = (f32[768]{0:T(1024)}, f32[768]{0:T(1024)}, f32[1024]{0:T(1024)S(1)}, f32[1024]{0:T(1024)S(1)}, f32[768]{0:T(1024)}, /*index=5*/f32[768]{0:T(1024)S(1)}, f32[1024,768]{1,0:T(8,128)S(1)}) fusion(f32[1024]{0:T(1024)S(1)} %add_rsqrt_fusion, f32[1024]{0:T(1024)S(1)} %broadcast_multiply_fusion.2, bf16[1024,1664]{1,0:T(8,128)(2,1)S(1)} %copy-done, ...), kind=kOutput, calls=%fused_computation.26 | convolution fusion | flops 313781248 | bytes 8686592 | tf_op jit(solution)/shard_map/dot_general | solution.py:18
  131.5 1.9 fusion.18
  133.4 3.4 %reshape.203 = bf16[8,128,2,384]{3,2,1,0:T(2,128)(2,1)S(1)} reshape(bf16[1024,768]{1,0:T(8,128)(2,1)} %fusion.18) | data formatting | bytes 3145728 | tf_op jit(solution)/shard_map/reshape | solution.py:59
  136.8 1.4 copy.93
  138.5 1.6 fusion.46
  140.1 1.9 add_convert_fusion
  142.0 0.4 reshape.201
  142.4 1.4 copy.91
  144.4 39.4 %psum.7 = f32[9984]{0:T(1024)S(1)} all-reduce(f32[9984]{0:T(1024)S(1)} %constant_dynamic-update-slice_fusion.5), channel_id=1, replica_groups=mesh['dp'=2,'ctx'=8,'tp'=2] {'dp','ctx','tp'}, use_global_device_ids=true, to_apply=%region_16.17 | all-reduce | flops 9984 | bytes 79872 | tf_op jit(solution)/shard_map/psum | solution.py:207
  183.9 5.1 %all-to-all-start.1 = ((bf16[8,48,640]{2,1,0:T(8,128)(2,1)}), bf16[8,48,640]{2,1,0:T(8,128)(2,1)S(1)}, u32[]{:S(2)}, u32[]{:S(2)}) async-start(bf16[8,48,640]{2,1,0:T(8,128)(2,1)} %bitcast.72), calls=%async_computation.4 | async-start | bytes 983040 | tf_op jit(solution)/shard_map/all_to_all | solution.py:54
  189.2 0.6 slice.181
  189.8 0.7 reshape.212
  190.4 0.6 fusion.97
  191.1 18.8 %reduce-scatter.6.cloned.1.call-done = bf16[1,128,384]{2,1,0:T(8,128)(2,1)} async-done(((bf16[16,128,384]{2,1,0:T(8,128)(2,1)}), bf16[1,128,384]{2,1,0:T(8,128)(2,1)}) %reduce-scatter.6.cloned.1.call-update) | async-done | bytes 98320 | tf_op jit(solution)/shard_map/reduce_scatter | solution.py:61
  209.9 1.6 convert_add_fusion
  211.4 60.0 %reduce-scatter.4.cloned.1.call-done = bf16[1,128,384]{2,1,0:T(8,128)(2,1)} async-done(((bf16[16,128,384]{2,1,0:T(8,128)(2,1)}), bf16[1,128,384]{2,1,0:T(8,128)(2,1)}) %reduce-scatter.4.cloned.1.call-update) | async-done | bytes 98320 | tf_op jit(solution)/shard_map/reduce_scatter | solution.py:61
  271.4 1.6 add_add_fusion
  273.4 0.2 copy.101
  273.6 0.9 reshape.211
  274.5 0.2 copy.102
  274.7 0.9 reshape.213
  275.6 0.2 reshape.205
  275.8 0.3 copy.98
  276.4 0.7 slice.178
  277.2 0.6 slice.183
  (114 shorter events, 3.9 us)
Async XLA Ops:
  7.2 4.5 %copy-start.7 = (bf16[48,1536]{1,0:T(8,128)(2,1)S(1)}, bf16[48,1536]{1,0:T(8,128)(2,1)}, u32[]{:S(2)}) copy-start(bf16[48,1536]{1,0:T(8,128)(2,1)} %param.24) | copy-start | bytes 442372
  7.2 4.7 %copy-start.8 = (bf16[48,1536]{1,0:T(8,128)(2,1)S(1)}, bf16[48,1536]{1,0:T(8,128)(2,1)}, u32[]{:S(2)}) copy-start(bf16[48,1536]{1,0:T(8,128)(2,1)} %param.26) | copy-start | bytes 442372
  7.2 4.8 %copy-start.9 = (bf16[48,384]{1,0:T(8,128)(2,1)S(1)}, bf16[48,384]{1,0:T(8,128)(2,1)}, u32[]{:S(2)}) copy-start(bf16[48,384]{1,0:T(8,128)(2,1)} %param.22) | copy-start | bytes 110596
  7.2 78.7 %all-gather.3.cloned.1.call-start = ((), (), s32[]{:S(2)}) async-start(), calls=%async_computation.5 | async-start | bytes 3833856 | tf_op jit(solution)/shard_map/all_gather | solution.py:43
  10.9 9.7 %copy-start.10 = (f32[3,384]{1,0:T(4,128)S(1)}, f32[3,384]{1,0:T(4,128)}, u32[]{:S(2)}) copy-start(f32[3,384]{1,0:T(4,128)} %param.21) | copy-start | bytes 13828
  12.4 77.4 %copy-start.17 = (f32[768]{0:T(1024)S(1)}, f32[768]{0:T(1024)}, u32[]{:S(2)}) copy-start(f32[768]{0:T(1024)} %param.17) | copy-start | bytes 9220
  12.4 77.4 %copy-start.20 = (f32[768]{0:T(1024)S(1)}, f32[768]{0:T(1024)}, u32[]{:S(2)}) copy-start(f32[768]{0:T(1024)} %param.16) | copy-start | bytes 9220
  13.3 32.9 %all-to-all-start = ((bf16[8,48,640]{2,1,0:T(8,128)(2,1)}), bf16[8,48,640]{2,1,0:T(8,128)(2,1)S(1)}, u32[]{:S(2)}, u32[]{:S(2)}) async-start(bf16[8,48,640]{2,1,0:T(8,128)(2,1)} %copy.90), calls=%async_computation | async-start | bytes 983040 | tf_op jit(solution)/shard_map/all_to_all | solution.py:47
  20.5 163.4 %reduce-scatter.8.cloned.1.call-start = ((), (), s32[]{:S(2)}) async-start(), calls=%async_computation.8 | async-start | bytes 1474560 | tf_op jit(solution)/shard_map/reduce_scatter | solution.py:53
  85.9 3.8 %copy-start.1 = (bf16[16,48,640]{2,1,0:T(8,128)(2,1)S(1)}, bf16[16,48,640]{2,1,0:T(8,128)(2,1)}, u32[]{:S(2)}) copy-start(bf16[16,48,640]{2,1,0:T(8,128)(2,1)} %all-gather) | copy-start | bytes 2949124
  89.8 2.8 copy-start
  98.1 2.9 %copy-start.18 = (f32[768]{0:T(1024)S(1)}, f32[768]{0:T(1024)}, u32[]{:S(2)}) copy-start(f32[768]{0:T(1024)} %param.17) | copy-start | bytes 9220
  98.1 2.9 %copy-start.21 = (f32[768]{0:T(1024)S(1)}, f32[768]{0:T(1024)}, u32[]{:S(2)}) copy-start(f32[768]{0:T(1024)} %param.16) | copy-start | bytes 9220
  100.3 0.8 copy-start.2
  101.0 3.5 %copy-start.15 = (f32[192]{0:T(256)S(1)}, f32[192]{0:T(256)}, u32[]{:S(2)}) copy-start(f32[192]{0:T(256)} %dynamic_slice.22) | copy-start | bytes 2308
  101.0 3.5 %copy-start.19 = (f32[768]{0:T(1024)S(1)}, f32[768]{0:T(1024)}, u32[]{:S(2)}) copy-start(f32[768]{0:T(1024)} %param.19) | copy-start | bytes 9220
  108.9 3.6 %copy-start.23 = (f32[768]{0:T(1024)S(1)}, f32[768]{0:T(1024)}, u32[]{:S(2)}) copy-start(f32[768]{0:T(1024)} %param.18) | copy-start | bytes 9220
  111.8 0.8 copy-start.24
  122.9 4.6 %copy-start.22 = (f32[768]{0:T(1024)S(1)}, f32[768]{0:T(1024)}, u32[]{:S(2)}) copy-start(f32[768]{0:T(1024)} %param.16) | copy-start | bytes 9220
  125.6 84.3 %reduce-scatter.6.cloned.1.call-start = ((), (), s32[]{:S(2)}) async-start(), calls=%async_computation.7 | async-start | bytes 1671168 | tf_op jit(solution)/shard_map/reduce_scatter | solution.py:61
  125.7 1.8 copy-start.25
  136.8 1.6 copy-start.14
  136.8 1.6 copy-start.4
  138.2 1.8 copy-start.6
  138.3 133.1 %reduce-scatter.4.cloned.1.call-start = ((), (), s32[]{:S(2)}) async-start(), calls=%async_computation.6 | async-start | bytes 1671168 | tf_op jit(solution)/shard_map/reduce_scatter | solution.py:61
  142.4 1.6 copy-start.3
  142.4 1.7 copy-start.16
  142.4 1.9 copy-start.13
  142.4 1.9 copy-start.12
  142.4 1.9 copy-start.11
  142.4 129.0 %copy-start.5 = (bf16[1,128,768]{2,1,0:T(8,128)(2,1)S(1)}, bf16[1,128,768]{2,1,0:T(8,128)(2,1)}, u32[]{:S(2)}) copy-start(bf16[1,128,768]{2,1,0:T(8,128)(2,1)} %param.14) | copy-start | bytes 589828
  183.9 89.1 %all-to-all-start.1 = ((bf16[8,48,640]{2,1,0:T(8,128)(2,1)}), bf16[8,48,640]{2,1,0:T(8,128)(2,1)S(1)}, u32[]{:S(2)}, u32[]{:S(2)}) async-start(bf16[8,48,640]{2,1,0:T(8,128)(2,1)} %bitcast.72), calls=%async_computation.4 | async-start | bytes 983040 | tf_op jit(solution)/shard_map/all_to_all | solution.py:54
Sparse Core Ops, SparseCore 0:
  10.2 75.6 all-gather.2
  125.7 18.1 reduce-scatter.7
  148.0 61.7 reduce-scatter.5
  213.4 57.9 reduce-scatter.3

commit v2 on v1

--- a/solution.py
+++ b/solution.py
@@ -1,8 +1,11 @@
+import functools
 import math
 
 import jax
 import jax.numpy as jnp
 from jax import lax
+from jax.experimental import pallas as pl
+from jax.experimental.pallas import tpu as pltpu
 from jax.sharding import PartitionSpec as P
 
 HD = 64
@@ -39,26 +42,311 @@
     )
 
 
-def gather_tokens(packed):
-    return lax.all_gather(packed, "ctx", axis=0, tiled=True)
-
-
-def weights_to_columns(blocks):
-    received = lax.all_to_all(blocks, "ctx", 0, 0, tiled=True)
-    return lax.all_gather(received, "dp", axis=0, tiled=False)
-
-
-def grads_to_owners(blocks):
-    dp, ctx = blocks.shape[:2]
-    mine = lax.psum_scatter(blocks, "dp", scatter_dimension=0, tiled=False)
-    return lax.all_to_all(mine, "ctx", 0, 0, tiled=True)
-
-
-def scatter_sum(partial, ctx, tp):
-    rows, width = partial.shape
-    parts = partial.reshape(ctx, rows // ctx, tp, width // tp).transpose(0, 2, 1, 3)
-    parts = parts.reshape(ctx * tp, rows // ctx, width // tp)
-    return lax.psum_scatter(parts, ("ctx", "tp"), scatter_dimension=0, tiled=False)
+MESH = pl.DeviceIdType.MESH
+INNER = 2
+
+
+def greet(ctx, dp, tp, my_ctx, my_dp, my_tp):
+    barrier = pltpu.get_barrier_semaphore()
+    for step in range(1, ctx):
+        peer = {"ctx": lax.rem(my_ctx + step, ctx)}
+        pl.semaphore_signal(barrier, inc=1, device_id=peer, device_id_type=MESH)
+    for step in range(1, dp):
+        peer = {"dp": lax.rem(my_dp + step, dp)}
+        pl.semaphore_signal(barrier, inc=1, device_id=peer, device_id_type=MESH)
+    for step in range(1, tp):
+        peer = {"tp": lax.rem(my_tp + step, tp)}
+        pl.semaphore_signal(barrier, inc=1, device_id=peer, device_id_type=MESH)
+    pl.semaphore_wait(barrier, ctx + dp + tp - 3)
+
+
+class Copies:
+    def __init__(self, send_sems, recv_sems):
+        self.send_sems, self.recv_sems, self.items = send_sems, recv_sems, []
+
+    def start(self, src, dst, peer):
+        place = len(self.items)
+        copy = pltpu.make_async_remote_copy(
+            src_ref=src,
+            dst_ref=dst,
+            send_sem=self.send_sems.at[place],
+            recv_sem=self.recv_sems.at[place],
+            device_id=peer,
+            device_id_type=MESH,
+        )
+        copy.start()
+        self.items.append(copy)
+        return copy
+
+    def finish(self):
+        for copy in self.items:
+            copy.wait_send()
+
+
+def gather_kernel(
+    ctx, dp, tp, packed, blocks, row, columns, send_sems, recv_sems, local_sems
+):
+    my_ctx, my_dp, my_tp = lax.axis_index("ctx"), lax.axis_index("dp"), lax.axis_index("tp")
+    outer = ctx // INNER
+    my_z, my_x = my_ctx // INNER, lax.rem(my_ctx, INNER)
+    rows = packed.shape[0]
+    half = rows // tp
+
+    def piece(owner, core):
+        return row.at[pl.ds(pl.multiple_of(owner * rows + core * half, half), half)]
+
+    own_row = pltpu.make_async_copy(
+        packed, row.at[pl.ds(pl.multiple_of(my_ctx * rows, rows), rows)], local_sems.at[0]
+    )
+    own_block = pltpu.make_async_copy(
+        blocks.at[my_ctx], columns.at[my_dp, my_ctx], local_sems.at[1]
+    )
+    own_row.start()
+    own_block.start()
+    greet(ctx, dp, tp, my_ctx, my_dp, my_tp)
+    copies = Copies(send_sems, recv_sems)
+    mine = packed.at[pl.ds(pl.multiple_of(my_tp * half, half), half)]
+    partner = {"ctx": my_z * INNER + (INNER - 1 - my_x)}
+    sibling = {"tp": tp - 1 - my_tp}
+    along = []
+    for step in range(1, outer):
+        target = lax.rem(my_z + step, outer) * INNER + my_x
+        along.append(copies.start(mine, piece(my_ctx, my_tp), {"ctx": target}))
+    across = [copies.start(mine, piece(my_ctx, my_tp), partner)]
+    exchanged = []
+    for step in range(1, ctx):
+        target = lax.rem(my_ctx + step, ctx)
+        exchanged.append(
+            copies.start(blocks.at[target], columns.at[my_dp, my_ctx], {"ctx": target})
+        )
+    to_sibling = []
+    for step in range(1, outer):
+        source = lax.rem(my_z + outer - step, outer) * INNER + my_x
+        along[step - 1].wait_recv()
+        across.append(copies.start(piece(source, my_tp), piece(source, my_tp), partner))
+        to_sibling.append(copies.start(piece(source, my_tp), piece(source, my_tp), sibling))
+    over_dp = []
+    for other in range(1, dp):
+        target = {"dp": lax.rem(my_dp + other, dp)}
+        over_dp.append(
+            copies.start(blocks.at[my_ctx], columns.at[my_dp, my_ctx], target)
+        )
+    for step in range(1, ctx):
+        source = lax.rem(my_ctx + ctx - step, ctx)
+        exchanged[step - 1].wait_recv()
+        for other in range(1, dp):
+            target = {"dp": lax.rem(my_dp + other, dp)}
+            over_dp.append(
+                copies.start(columns.at[my_dp, source], columns.at[my_dp, source], target)
+            )
+    for step in range(outer):
+        source = lax.rem(my_z + outer - step, outer) * INNER + (INNER - 1 - my_x)
+        across[step].wait_recv()
+        to_sibling.append(copies.start(piece(source, my_tp), piece(source, my_tp), sibling))
+    for copy in over_dp + to_sibling:
+        copy.wait_recv()
+    copies.finish()
+    own_row.wait()
+    own_block.wait()
+
+
+def gather_all(packed, blocks, dp, ctx, tp):
+    outer = ctx // INNER
+    count = (outer - 1) + outer + (ctx - 1) + (2 * outer - 1) + ctx * (dp - 1)
+    return pl.pallas_call(
+        functools.partial(gather_kernel, ctx, dp, tp),
+        out_shape=(
+            jax.ShapeDtypeStruct((ctx * packed.shape[0], packed.shape[1]), packed.dtype),
+            jax.ShapeDtypeStruct((dp,) + blocks.shape, blocks.dtype),
+        ),
+        in_specs=[pl.BlockSpec(memory_space=pl.ANY)] * 2,
+        out_specs=(pl.BlockSpec(memory_space=pl.ANY),) * 2,
+        scratch_shapes=[
+            pltpu.SemaphoreType.DMA((count,)),
+            pltpu.SemaphoreType.DMA((count,)),
+            pltpu.SemaphoreType.DMA((2,)),
+        ],
+        compiler_params=pltpu.CompilerParams(collective_id=0, has_side_effects=True),
+    )(packed, blocks)
+
+
+def reduce_kernel(
+    ctx,
+    dp,
+    tp,
+    partial,
+    grads,
+    vectors,
+    sums,
+    own_grads,
+    totals,
+    from_core,
+    to_x,
+    from_x,
+    to_z,
+    from_z,
+    from_y,
+    summed,
+    core_vector,
+    x_vector,
+    passed_vector,
+    z_vectors,
+    y_vectors,
+    send_sems,
+    recv_sems,
+    local_sem,
+):
+    f32, bf16 = jnp.float32, jnp.bfloat16
+    my_ctx, my_dp, my_tp = lax.axis_index("ctx"), lax.axis_index("dp"), lax.axis_index("tp")
+    outer = ctx // INNER
+    my_z, my_x = my_ctx // INNER, lax.rem(my_ctx, INNER)
+    rows = sums.shape[0]
+    greet(ctx, dp, tp, my_ctx, my_dp, my_tp)
+    copies = Copies(send_sems, recv_sems)
+    partner = {"ctx": my_z * INNER + (INNER - 1 - my_x)}
+    sibling = {"tp": tp - 1 - my_tp}
+    other_core = tp - 1 - my_tp
+
+    def group(step):
+        first = lax.rem(my_z + step, outer) * INNER * rows
+        return pl.ds(pl.multiple_of(first, rows), INNER * rows)
+
+    def token_rows(step, x):
+        first = (lax.rem(my_z + step, outer) * INNER + x) * rows
+        return pl.ds(pl.multiple_of(first, rows), rows)
+
+    vector_core = copies.start(vectors, core_vector, sibling)
+    order = list(range(1, outer)) + [0]
+    over_core = {}
+    for step in order:
+        here = group(step)
+        over_core[step] = copies.start(
+            partial.at[other_core, here], from_core.at[here], sibling
+        )
+    over_y = []
+    for other in range(1, dp):
+        target = lax.rem(my_dp + other, dp)
+        over_y.append(copies.start(grads.at[target], from_y.at[other - 1], {"dp": target}))
+
+    over_x = {}
+    for step in order:
+        over_core[step].wait_recv()
+        there = token_rows(step, INNER - 1 - my_x)
+        to_x[step] = (
+            partial[my_tp, there, :].astype(f32) + from_core[there, :].astype(f32)
+        ).astype(bf16)
+        over_x[step] = copies.start(to_x.at[step], from_x.at[step], partner)
+
+    vector_core.wait_recv()
+    passed_vector[0] = vectors[...] + core_vector[...]
+    vector_x = copies.start(passed_vector.at[0], x_vector, partner)
+
+    def own_sum(step):
+        here = token_rows(step, my_x)
+        local = partial[my_tp, here, :].astype(f32) + from_core[here, :].astype(f32)
+        return local + from_x[step].astype(f32)
+
+    over_z = {}
+    for step in range(1, outer):
+        over_x[step].wait_recv()
+        to_z[step - 1] = own_sum(step).astype(bf16)
+        target = lax.rem(my_z + step, outer) * INNER + my_x
+        over_z[step] = copies.start(to_z.at[step - 1], from_z.at[step - 1], {"ctx": target})
+
+    vector_x.wait_recv()
+    passed_vector[1] = passed_vector[0] + x_vector[...]
+    z_vectors[my_z] = passed_vector[1]
+    vector_z = []
+    for step in range(1, outer):
+        target = lax.rem(my_z + step, outer) * INNER + my_x
+        vector_z.append(
+            copies.start(passed_vector.at[1], z_vectors.at[my_z], {"ctx": target})
+        )
+
+    for copy in over_y:
+        copy.wait_recv()
+    over_ctx = []
+    for step in list(range(1, ctx)) + [0]:
+        target = lax.rem(my_ctx + step, ctx)
+        total = grads[my_dp, target].astype(f32)
+        for other in range(1, dp):
+            total = total + from_y[other - 1, target].astype(f32)
+        summed[step] = total.astype(bf16)
+        if step > 0:
+            over_ctx.append(
+                copies.start(summed.at[step], own_grads.at[my_ctx], {"ctx": target})
+            )
+    own = pltpu.make_async_copy(summed.at[0], own_grads.at[my_ctx], local_sem)
+    own.start()
+
+    for copy in vector_z:
+        copy.wait_recv()
+    total = z_vectors[0]
+    for place in range(1, outer):
+        total = total + z_vectors[place]
+    passed_vector[2] = total
+    y_vectors[my_dp] = total
+    vector_y = []
+    for other in range(1, dp):
+        target = {"dp": lax.rem(my_dp + other, dp)}
+        vector_y.append(copies.start(passed_vector.at[2], y_vectors.at[my_dp], target))
+
+    over_x[0].wait_recv()
+    result = own_sum(0)
+    for step in range(1, outer):
+        over_z[step].wait_recv()
+        result = result + from_z[step - 1].astype(f32)
+    sums[...] = result
+    for copy in vector_y:
+        copy.wait_recv()
+    total = y_vectors[0]
+    for place in range(1, dp):
+        total = total + y_vectors[place]
+    totals[...] = total
+    for copy in over_ctx:
+        copy.wait_recv()
+    copies.finish()
+    own.wait()
+
+
+def reduce_all(partial, grads, vectors, dp, ctx, tp):
+    outer = ctx // INNER
+    rows, width = partial.shape[1] // ctx, partial.shape[2]
+    block = grads.shape[2:]
+    bf16 = jnp.bfloat16
+    count = outer + (dp - 1) + outer + (outer - 1) + (ctx - 1)
+    count += 2 + (outer - 1) + (dp - 1)
+    vmem = pl.BlockSpec(memory_space=pltpu.VMEM)
+    return pl.pallas_call(
+        functools.partial(reduce_kernel, ctx, dp, tp),
+        out_shape=(
+            jax.ShapeDtypeStruct((rows, width), jnp.float32),
+            jax.ShapeDtypeStruct((ctx,) + block, bf16),
+            jax.ShapeDtypeStruct(vectors.shape, jnp.float32),
+        ),
+        in_specs=[vmem] * 3,
+        out_specs=(vmem, pl.BlockSpec(memory_space=pl.ANY), vmem),
+        scratch_shapes=[
+            pltpu.VMEM(partial.shape[1:], bf16),
+            pltpu.VMEM((outer, rows, width), bf16),
+            pltpu.VMEM((outer, rows, width), bf16),
+            pltpu.VMEM((outer - 1, rows, width), bf16),
+            pltpu.VMEM((outer - 1, rows, width), bf16),
+            pltpu.VMEM((dp - 1, ctx) + block, bf16),
+            pltpu.VMEM((ctx,) + block, bf16),
+            pltpu.VMEM(vectors.shape, jnp.float32),
+            pltpu.VMEM(vectors.shape, jnp.float32),
+            pltpu.VMEM((3,) + vectors.shape, jnp.float32),
+            pltpu.VMEM((outer,) + vectors.shape, jnp.float32),
+            pltpu.VMEM((dp,) + vectors.shape, jnp.float32),
+            pltpu.SemaphoreType.DMA((count,)),
+            pltpu.SemaphoreType.DMA((count,)),
+            pltpu.SemaphoreType.DMA,
+        ],
+        compiler_params=pltpu.CompilerParams(
+            collective_id=1, has_side_effects=True, vmem_limit_bytes=48 * 2**20
+        ),
+    )(partial, grads, vectors)
 
 
 def on_device(
@@ -102,15 +390,18 @@
         ],
         axis=-1,
     )
-    columns = weights_to_columns(blocks).reshape(width, -1)
+    block_width = blocks.shape[-1]
+    pad_rows, pad_width = -owned % 16, -block_width % 128
+    blocks = jnp.pad(blocks, ((0, 0), (0, pad_rows), (0, pad_width)))
+    seg_columns = jnp.broadcast_to(segments[0].astype(bf16)[:, None], (local_rows, 128))
+    packed = jnp.concatenate([inputs[0], cotangent[0], seg_columns], axis=-1)
+    row, columns = gather_all(packed, blocks, dp, ctx, tp)
+    columns = columns[:, :, :owned, :block_width].reshape(width, -1)
     up = columns[:, :units]
     down = columns[:, units : 2 * units]
     qkv = columns[:, 2 * units : 2 * units + 3 * head_width]
     out = columns[:, 2 * units + 3 * head_width :]
 
-    seg_columns = jnp.broadcast_to(segments[0].astype(bf16)[:, None], (local_rows, 128))
-    packed = jnp.concatenate([inputs[0], cotangent[0], seg_columns], axis=-1)
-    row = gather_tokens(packed)
     tokens = row[:, :width].astype(f32)
     grad_out = row[:, width : 2 * width]
     seg = row[:, 2 * width]
@@ -149,7 +440,6 @@
     pre_gelu = dot_f32(norm_two, up) + up_bias
     activated = jax.nn.gelu(pre_gelu, approximate=False).astype(bf16)
     branch = dot_f32(attended_low, out, LAST) + dot_f32(activated, down, LAST)
-    branch_share = scatter_sum(branch.astype(bf16), ctx, tp).astype(f32)
 
     grad_attended = dot_f32(grad_out, out).astype(bf16)
     grad_activated = dot_f32(grad_out, down)
@@ -187,11 +477,43 @@
         - jnp.mean(pulled, axis=-1, keepdims=True)
         - xhat * jnp.mean(pulled * xhat, axis=-1, keepdims=True)
     )
-    input_share = scatter_sum(input_term.astype(bf16), ctx, tp).astype(f32)
 
     grads = jnp.concatenate([grad_w_up, grad_w_down, grad_w_qkv, grad_w_out], axis=-1)
     grads = grads.astype(bf16).reshape(dp, ctx, owned, -1)
-    own = grads_to_owners(grads).astype(f32)
+    grads = jnp.pad(grads, ((0, 0), (0, 0), (0, pad_rows), (0, pad_width)))
+
+    grad_bias = jnp.sum(cotangent[0].astype(f32), axis=0) * (my_tp == 0).astype(f32)
+    place = (jnp.arange(tp)[:, None] == my_tp) & (jnp.arange(ctx)[None, :] == my_ctx)
+    local = jnp.concatenate([grad_b_qkv, grad_b_up])
+    spread = jnp.where(place[:, :, None], local, 0.0)
+    vectors = jnp.concatenate(
+        [
+            grad_gain_one,
+            grad_bias_one,
+            grad_gain_two,
+            grad_bias_two,
+            grad_bias,
+            spread.reshape(-1),
+        ]
+    )
+    vector_size = vectors.shape[0]
+    vectors = jnp.pad(vectors, (0, -vector_size % 1024)).reshape(-1, 128)
+    branch_low, input_low = branch.astype(bf16), input_term.astype(bf16)
+    partial = jnp.stack(
+        [
+            jnp.concatenate(
+                [
+                    branch_low[:, part * share : (part + 1) * share],
+                    input_low[:, part * share : (part + 1) * share],
+                ],
+                axis=-1,
+            )
+            for part in range(tp)
+        ]
+    )
+    sums, own, total = reduce_all(partial, grads, vectors, dp, ctx, tp)
+    branch_share, input_share = sums[:, :share], sums[:, share:]
+    own = own[:, :owned, :block_width].astype(f32)
     own_up = own[:, :, :units].transpose(1, 0, 2).reshape(owned, -1)
     own_down = own[:, :, units : 2 * units].transpose(1, 0, 2).reshape(owned, -1)
     own_qkv = own[:, :, 2 * units : 2 * units + 3 * head_width]
@@ -199,24 +521,7 @@
     own_qkv = own_qkv.reshape(owned, 3, ctx * head_width)[:, :, : heads * HD]
     own_out = own[:, :, 2 * units + 3 * head_width :].transpose(1, 0, 2)
     own_out = own_out.reshape(owned, -1)[:, : heads * HD]
-
-    grad_bias = jnp.sum(cotangent[0].astype(f32), axis=0) * (my_tp == 0).astype(f32)
-    place = (jnp.arange(tp)[:, None] == my_tp) & (jnp.arange(ctx)[None, :] == my_ctx)
-    local = jnp.concatenate([grad_b_qkv, grad_b_up])
-    spread = jnp.where(place[:, :, None], local, 0.0)
-    total = lax.psum(
-        jnp.concatenate(
-            [
-                grad_gain_one,
-                grad_bias_one,
-                grad_gain_two,
-                grad_bias_two,
-                grad_bias,
-                spread.reshape(-1),
-            ]
-        ),
-        ("dp", "ctx", "tp"),
-    )
+    total = total.reshape(-1)[:vector_size]
     spread = total[5 * width :].reshape(tp, ctx, -1)
     spread = lax.dynamic_index_in_dim(spread, my_tp, 0, keepdims=False)
     sum_b_qkv = spread[:, : 3 * head_width].reshape(ctx, 3, head_width).transpose(1, 0, 2)

time: 285 us -> 167 us (0.59)
  waiting for transfers between devices: 133 us -> 0 us
  Pallas kernels: 0 us -> 84.5 us
  blocking collectives: 49 us -> 0 us
  between operations: 14.4 us -> 1.23 us
  starting transfers between devices: 12.5 us -> 0 us
  other arithmetic: 17.2 us -> 21.3 us
    pallas_call x0 -> x2, Pallas kernels: none -> 84.5 us  [the longest x1 42.8 us: reduce_all(): pl.pallas_call(functools.partial(reduce_kernel, ctx, dp, tp), out_shape=(...]
    reduce_scatter x3 -> x0, waiting for transfers between devices: 78.8 us -> none  [the longest x2 78.8 us: scatter_sum(): lax.psum_scatter(parts, ('ctx', 'tp'), scatter_dimension=0, tiled=False)]
    psum x1 -> x0, blocking collectives: 39.4 us -> none  [on_device(): lax.psum(jnp.concatenate([grad_gain_one, grad_bias_one, grad_gain_two, gr...]
    all_gather x1 -> x0, waiting for transfers between devices: 30.2 us -> none  [gather_tokens(): return lax.all_gather(packed, 'ctx', axis=0, tiled=True)]
    all_to_all x2 -> x0, waiting for transfers between devices: 24 us -> none  [the longest x1 24 us: weights_to_columns(): received = lax.all_to_all(blocks, 'ctx', 0, 0, tiled=True)]
    all_to_all x2 -> x0, starting transfers between devices: 12.3 us -> none  [the longest x1 7.25 us: weights_to_columns(): received = lax.all_to_all(blocks, 'ctx', 0, 0, tiled=True)]
    all_gather x1 -> x0, blocking collectives: 9.6 us -> none  [weights_to_columns(): return lax.all_gather(received, 'dp', axis=0, tiled=False)]
    dot_general x0 -> x2, local copies, waits for them, and re-layouts: none -> 7.32 us  [dot_f32(): return lax.dot_general(a, b, dims, preferred_element_type=jnp.float32)]
  transfers between devices with their start and end apart: 6 -> 0, of which waited for: 4 -> 0; matrix products, arithmetic and copies ran while one was open for 10% -> 0% of each run, Pallas kernels for 0% -> 0%
where the time goes in v2:
time: 167 us; the launch traced here: 165 us
  Pallas kernels  84.5 us (51%)
  matrix products  30.9 us (19%)
  local copies, waits for them, and re-layouts  27 us (16%)
  other arithmetic  21.3 us (13%)
    pallas_call x1, Pallas kernels, reduce_all(): pl.pallas_call(functools.partial(reduce_kernel, ctx, dp, tp), out_shape=(...  42.8 us
    pallas_call x1, Pallas kernels, gather_all(): pl.pallas_call(functools.partial(gather_kernel, ctx, dp, tp), out_shape=(...  41.7 us
    dot_general x18, matrix products, dot_f32(): return lax.dot_general(a, b, dims, preferred_element_type=jnp.float32)  30.9 us
    dot_general x2, local copies, waits for them, and re-layouts, dot_f32(): return lax.dot_general(a, b, dims, preferred_element_type=jnp.float32)  7.32 us
    another operation x4, local copies, waits for them, and re-layouts  6.45 us
    reduce_sum x1, other arithmetic, on_device(): grad_gain_two = jnp.sum(grad_norm_two * xhat, axis=0)  5.77 us

profile of v2, /device:TPU:0, one launch (start us, length us, event | category | flops | bytes accessed | tf_op | source)
XLA Modules:
  0.0 165.0 jit_solution(12981604550906289497)
XLA Ops:
  0.7 1.2 reshape.192
  1.9 1.1 reshape.193
  3.1 0.9 pad.16
  4.0 0.2 reshape.194
  4.2 0.3 copy.85
  4.4 0.2 reshape.195
  4.9 1.0 pad_maximum_fusion.2.blocks
  6.0 0.8 pad_maximum_fusion.3.packed
  6.8 41.7 %shard_map.237 = (bf16[1024,1664]{1,0:T(8,128)(2,1)}, bf16[2,8,48,640]{3,2,1,0:T(8,128)(2,1)}) custom-call(bf16[128,1664]{1,0:T(8,128)(2,1)} %pad_maximum_fusion.3.packed, bf16[8,48,640]{2,1,0:T(8,128)(2,1)} %pad_maximum_fusion.2.blocks), custom_call_target="tpu_custom_call" | custom-call | tf_op jit(solution)/shard_map/pallas_call | solution.py:156
  48.5 1.7 %convert_reduce_fusion = f32[1024]{0:T(1024)S(1)} fusion(bf16[1024,1664]{1,0:T(8,128)(2,1)} %get-tuple-element.18), kind=kLoop, calls=%fused_computation.6 | loop fusion | flops 1571840 | bytes 1576960 | tf_op jit(solution)/shard_map/reduce_sum | solution.py:413
  50.2 2.0 %fusion.21 = f32[1024]{0:T(1024)S(1)} fusion(f32[1024]{0:T(1024)S(1)} %broadcast_multiply_fusion.2, bf16[1024,1664]{1,0:T(8,128)(2,1)} %get-tuple-element.18), kind=kLoop, calls=%fused_computation.27 | loop fusion | flops 3144704 | bytes 1581056 | tf_op jit(solution)/shard_map/reduce_sum | solution.py:415
  52.5 2.6 %fusion.103 = (bf16[1024,192]{0,1:T(8,128)(2,1)S(1)}, f32[1024,192]{0,1:T(8,128)S(1)}) fusion(f32[192]{0:T(256)S(1)} %add.107, bf16[768,640]{1,0:T(8,128)(2,1)} %bitcast.77, f32[768]{0:T(1024)S(1)} %copy-done.17, f32[768]{0:T(1024)S(1)} %copy-done.14, f32[1024]{0:T(1024)S(1)} %add_rsqrt_fusion, f32[1024]{0:T(1024)S(1)} %broadcast_multiply_fusion.2, ...), kind=kOutput, calls=%fused_computation.181 | convolution fusion | flops 307101696 | bytes 3160832 | tf_op jit(solution)/shard_map/dot_general | solution.py:21
  55.1 0.2 fusion.84
  55.5 1.0 fusion.104
  56.5 0.6 fusion.10
  57.2 0.7 fusion.22
  57.9 0.5 copy-done.2
  58.4 0.7 convolution_convert_fusion.4
  59.0 1.2 multiply_reduce_fusion
  60.2 1.1 multiply_convert_fusion
  61.3 0.8 convolution_multiply_fusion.1
  62.0 0.5 convolution_multiply_fusion
  62.5 0.2 constant_dynamic-update-slice_fusion.3
  62.7 0.2 constant_dynamic-update-slice_fusion.2
  62.9 0.2 constant_dynamic-update-slice_fusion.1
  63.2 0.2 constant_dynamic-update-slice_fusion
  63.4 0.8 fusion.23
  64.2 2.3 %fusion.105 = (f32[768]{0:T(1024)S(1)}, f32[1024,768]{0,1:T(8,128)}) fusion(bf16[1024,192]{0,1:T(8,128)(2,1)S(1)} %fusion.23, bf16[768,640]{1,0:T(8,128)(2,1)S(1)} %bitcast.82), kind=kOutput, calls=%fused_computation.183 | convolution fusion | flops 302775552 | bytes 3935232 | tf_op jit(solution)/shard_map/dot_general | solution.py:21
  66.4 3.7 %copy.65 = f32[1024,768]{1,0:T(8,128)} copy(f32[1024,768]{0,1:T(8,128)} %get-tuple-element.59) | data formatting | bytes 6291456 | tf_op jit(solution)/shard_map/dot_general | solution.py:21
  70.2 0.8 dynamic_slice.22
  70.9 4.4 %multiply_convert_fusion.1 = (bf16[1024,192]{0,1:T(8,128)(2,1)}, f32[1024,192]{0,1:T(8,128)S(1)}, f32[1024,192]{0,1:T(8,128)S(1)}) fusion(f32[192]{0:T(256)S(1)} %dynamic_slice.22, bf16[768,640]{1,0:T(8,128)(2,1)} %bitcast.78, f32[768]{0:T(1024)S(1)} %copy-done.18, f32[768]{0:T(1024)S(1)} %copy-done.15, f32[1024]{0:T(1024)S(1)} %add_rsqrt_fusion, ...), kind=kOutput, calls=%fused_computation.56 | convolution fusion | flops 319684608 | bytes 3949568 | tf_op jit(solution)/shard_map/dot_general | solution.py:21
  75.4 1.1 convert_reduce_fusion.1
  76.5 2.3 %fusion.106 = (f32[768]{0:T(1024)S(1)}, f32[1024,768]{0,1:T(8,128)}) fusion(bf16[1024,192]{0,1:T(8,128)(2,1)S(1)} %get-tuple-element.63, bf16[768,640]{1,0:T(8,128)(2,1)S(1)} %bitcast.84), kind=kOutput, calls=%fused_computation.184 | convolution fusion | flops 302775552 | bytes 3935232 | tf_op jit(solution)/shard_map/dot_general | solution.py:21
  78.7 3.6 %copy.66 = f32[1024,768]{1,0:T(8,128)} copy(f32[1024,768]{0,1:T(8,128)} %get-tuple-element.61) | data formatting | bytes 6291456 | tf_op jit(solution)/shard_map/dot_general | solution.py:21
  82.3 5.8 %fusion.20 = (f32[768]{0:T(1024)S(1)}, f32[768]{0:T(1024)S(1)}, f32[1024]{0:T(1024)}, f32[1024]{0:T(1024)}, f32[1024,768]{1,0:T(8,128)}) fusion(f32[1024,768]{1,0:T(8,128)} %copy.66, f32[1024]{0:T(1024)S(1)} %add_rsqrt_fusion, f32[1024]{0:T(1024)S(1)} %broadcast_multiply_fusion.2, bf16[1024,1664]{1,0:T(8,128)(2,1)S(1)} %copy-done, f32[1024,768]{1,0:T(8,128)} %copy.65, ...), kind=kLoop, calls=%fused_computation.26 | loop fusion | flops 10220032 | bytes 11038720 | tf_op jit(solution)/shard_map/reduce_sum | solution.py:472
  88.1 1.0 convert_reduce_fusion.3
  89.1 1.1 convert_reduce_fusion.2
  90.5 2.6 %convolution_convert_fusion = bf16[768,192]{0,1:T(8,128)(2,1)} fusion(bf16[1024,192]{0,1:T(8,128)(2,1)} %copy-done.4, f32[768]{0:T(1024)S(1)} %copy-done.17, f32[768]{0:T(1024)S(1)} %copy-done.14, f32[1024]{0:T(1024)S(1)} %add_rsqrt_fusion, f32[1024]{0:T(1024)S(1)} %broadcast_multiply_fusion.2, bf16[1024,1664]{1,0:T(8,128)(2,1)S(1)} %copy-done), kind=kOutput, calls=%fused_computation.35 | convolution fusion | flops 306855936 | bytes 2277376 | tf_op jit(solution)/shard_map/dot_general | solution.py:21
  93.1 1.9 %copy.69 = bf16[768,192]{1,0:T(8,128)(2,1)} copy(bf16[768,192]{0,1:T(8,128)(2,1)} %convolution_convert_fusion) | data formatting | bytes 589824 | tf_op jit(solution)/shard_map/convert.7
  95.0 2.6 %convolution_convert_fusion.2 = bf16[768,192]{0,1:T(8,128)(2,1)} fusion(bf16[1024,192]{0,1:T(8,128)(2,1)} %copy-done.8, f32[768]{0:T(1024)S(1)} %copy-done.18, f32[768]{0:T(1024)S(1)} %copy-done.15, f32[1024]{0:T(1024)S(1)} %add_rsqrt_fusion, f32[1024]{0:T(1024)S(1)} %broadcast_multiply_fusion.2, bf16[1024,1664]{1,0:T(8,128)(2,1)S(1)} %copy-done), kind=kOutput, calls=%fused_computation.37 | convolution fusion | flops 306855936 | bytes 2277376 | tf_op jit(solution)/shard_map/dot_general | solution.py:21
  97.6 1.9 %copy.67 = bf16[768,192]{1,0:T(8,128)(2,1)} copy(bf16[768,192]{0,1:T(8,128)(2,1)} %convolution_convert_fusion.2) | data formatting | bytes 589824 | tf_op jit(solution)/shard_map/convert.9
  99.5 1.3 convolution_convert_fusion.5
  100.8 0.8 copy.70
  101.6 2.2 %convolution_convert_fusion.1 = bf16[768,192]{0,1:T(8,128)(2,1)} fusion(bf16[1024,192]{0,1:T(8,128)(2,1)} %get-tuple-element.27, bf16[1024,1664]{1,0:T(8,128)(2,1)S(1)} %copy-done), kind=kOutput, calls=%fused_computation.36 | convolution fusion | flops 302137344 | bytes 2260992 | tf_op jit(solution)/shard_map/dot_general | solution.py:21
  103.8 1.9 %copy.68 = bf16[768,192]{1,0:T(8,128)(2,1)} copy(bf16[768,192]{0,1:T(8,128)(2,1)} %convolution_convert_fusion.1) | data formatting | bytes 589824 | tf_op jit(solution)/shard_map/convert.8
  105.7 1.8 %pad_maximum_fusion.1.grads = bf16[2,8,48,640]{3,2,1,0:T(8,128)(2,1)S(1)} fusion(bf16[2,8,48,64]{3,2,1,0:T(8,128)(2,1)} %bitcast.90, bf16[2,8,48,192]{3,2,1,0:T(8,128)(2,1)} %bitcast.85, bf16[2,8,48,192]{3,2,1,0:T(8,128)(2,1)} %bitcast.87, bf16[2,8,48,192]{3,2,1,0:T(8,128)(2,1)} %bitcast.86), kind=kLoop, calls=%fused_computation.51 | loop fusion | flops 3932160 | bytes 1966080 | tf_op jit(solution)/shard_map/concatenate | solution.py:481
  107.5 1.7 %fusion.49 = f32[1024,768]{1,0:T(8,128)S(1)} fusion(bf16[768,640]{1,0:T(8,128)(2,1)} %bitcast.79, bf16[1024,64]{0,1:T(8,128)(2,1)} %get-tuple-element.57), kind=kOutput, calls=%fused_computation.97 | convolution fusion | flops 100663296 | bytes 3473408 | tf_op jit(solution)/shard_map/dot_general | solution.py:21
  109.2 2.0 %add_convert_fusion = bf16[1024,768]{1,0:T(8,128)(2,1)S(1)} fusion(f32[1024,768]{1,0:T(8,128)S(1)} %fusion.49, bf16[1024,192]{0,1:T(8,128)(2,1)S(1)} %copy-done.9, bf16[768,640]{1,0:T(8,128)(2,1)} %bitcast.80), kind=kOutput, calls=%fused_computation.30 | convolution fusion | flops 303562752 | bytes 5505024 | tf_op jit(solution)/shard_map/dot_general | solution.py:21
  111.4 1.3 fusion.18
  113.1 0.3 pad_maximum_fusion.partial
  113.4 42.8 %shard_map.238 = (f32[128,768]{1,0:T(8,128)S(1)}, bf16[8,48,640]{2,1,0:T(8,128)(2,1)S(1)}, f32[80,128]{1,0:T(8,128)S(1)}) custom-call(bf16[2,1024,768]{2,1,0:T(8,128)(2,1)S(1)} %pad_maximum_fusion.partial, bf16[2,8,48,640]{3,2,1,0:T(8,128)(2,1)S(1)} %pad_maximum_fusion.1.grads, f32[80,128]{1,0:T(8,128)S(1)} %pad_bitcast_fusion.vectors), custom_call_target="tpu_custom_call" | custom-call | tf_op jit(solution)/shard_map/pallas_call | solution.py:320
  156.4 0.2 copy.76
  156.7 0.9 reshape.206
  157.5 0.2 copy.77
  157.8 0.9 reshape.208
  158.7 0.2 reshape.200
  158.9 0.3 copy.73
  159.3 0.2 reshape.201
  159.5 0.7 slice.228
  160.5 0.6 slice.232
  161.2 1.7 %fusion.45 = (f32[1,128,384]{2,1,0:T(8,128)}, f32[1,128,384]{2,1,0:T(8,128)}) fusion(f32[128,768]{1,0:T(8,128)S(1)} %get-tuple-element.20, bf16[1,128,768]{2,1,0:T(8,128)(2,1)S(1)} %copy-done.6, s32[]{:T(128)S(6)} %select_n.28, f32[384]{0:T(512)S(1)} %dynamic_slice.23, bf16[1,128,768]{2,1,0:T(8,128)(2,1)} %param.14), kind=kLoop, calls=%fused_computation.90 | loop fusion | flops 245760 | bytes 984580 | tf_op jit(solution)/shard_map/broadcast_in_dim | solution.py:539
  163.1 0.6 slice.230
  163.7 0.7 reshape.207
  164.4 0.6 slice_bitcast_fusion.3
  (91 shorter events, 2.6 us)
Async XLA Ops:
  0.6 4.0 %copy-start.10 = (bf16[48,384]{1,0:T(8,128)(2,1)S(1)}, bf16[48,384]{1,0:T(8,128)(2,1)}, u32[]{:S(2)}) copy-start(bf16[48,384]{1,0:T(8,128)(2,1)} %param.22) | copy-start | bytes 110596
  0.7 5.2 %copy-start.19 = (s32[1,128]{1,0:T(1,128)S(1)}, s32[1,128]{1,0:T(1,128)}, u32[]{:S(2)}) copy-start(s32[1,128]{1,0:T(1,128)} %param.15) | copy-start | bytes 1540
  0.7 5.3 %copy-start.7 = (bf16[1,128,768]{2,1,0:T(8,128)(2,1)S(1)}, bf16[1,128,768]{2,1,0:T(8,128)(2,1)}, u32[]{:S(2)}) copy-start(bf16[1,128,768]{2,1,0:T(8,128)(2,1)} %param.14) | copy-start | bytes 589828
  0.7 5.3 %copy-start.5 = (bf16[1,128,768]{2,1,0:T(8,128)(2,1)S(1)}, bf16[1,128,768]{2,1,0:T(8,128)(2,1)}, u32[]{:S(2)}) copy-start(bf16[1,128,768]{2,1,0:T(8,128)(2,1)} %param.27) | copy-start | bytes 589828
  4.8 47.4 %copy-start.13 = (f32[3,384]{1,0:T(4,128)S(1)}, f32[3,384]{1,0:T(4,128)}, u32[]{:S(2)}) copy-start(f32[3,384]{1,0:T(4,128)} %param.21) | copy-start | bytes 13828
  4.8 47.6 %copy-start.14 = (f32[768]{0:T(1024)S(1)}, f32[768]{0:T(1024)}, u32[]{:S(2)}) copy-start(f32[768]{0:T(1024)} %param.16) | copy-start | bytes 9220
  4.9 47.6 %copy-start.17 = (f32[768]{0:T(1024)S(1)}, f32[768]{0:T(1024)}, u32[]{:S(2)}) copy-start(f32[768]{0:T(1024)} %param.17) | copy-start | bytes 9220
  52.5 2.9 %copy-start = (bf16[1024,1664]{1,0:T(8,128)(2,1)S(1)}, bf16[1024,1664]{1,0:T(8,128)(2,1)}, u32[]{:S(2)}) copy-start(bf16[1024,1664]{1,0:T(8,128)(2,1)} %get-tuple-element.18) | copy-start | bytes 10223620
  57.2 1.2 copy-start.2
  64.1 2.3 %copy-start.4 = (bf16[1024,192]{0,1:T(8,128)(2,1)}, bf16[1024,192]{0,1:T(8,128)(2,1)S(1)}, u32[]{:S(2)}) copy-start(bf16[1024,192]{0,1:T(8,128)(2,1)S(1)} %fusion.23) | copy-start | bytes 1179652
  66.4 4.5 %copy-start.15 = (f32[768]{0:T(1024)S(1)}, f32[768]{0:T(1024)}, u32[]{:S(2)}) copy-start(f32[768]{0:T(1024)} %param.18) | copy-start | bytes 9220
  66.4 4.5 %copy-start.18 = (f32[768]{0:T(1024)S(1)}, f32[768]{0:T(1024)}, u32[]{:S(2)}) copy-start(f32[768]{0:T(1024)} %param.19) | copy-start | bytes 9220
  70.9 4.4 %copy-start.3 = (bf16[2,8,48,640]{3,2,1,0:T(8,128)(2,1)S(1)}, bf16[2,8,48,640]{3,2,1,0:T(8,128)(2,1)}, u32[]{:S(2)}) copy-start(bf16[2,8,48,640]{3,2,1,0:T(8,128)(2,1)} %get-tuple-element.19) | copy-start | bytes 2949124
  76.4 2.3 %copy-start.8 = (bf16[1024,192]{0,1:T(8,128)(2,1)}, bf16[1024,192]{0,1:T(8,128)(2,1)S(1)}, u32[]{:S(2)}) copy-start(bf16[1024,192]{0,1:T(8,128)(2,1)S(1)} %get-tuple-element.63) | copy-start | bytes 1179652
  105.7 3.4 %copy-start.9 = (bf16[1024,192]{0,1:T(8,128)(2,1)S(1)}, bf16[1024,192]{0,1:T(8,128)(2,1)}, u32[]{:S(2)}) copy-start(bf16[1024,192]{0,1:T(8,128)(2,1)} %get-tuple-element.27) | copy-start | bytes 1179652
  109.1 2.2 %copy-start.12 = (f32[1024]{0:T(1024)S(1)}, f32[1024]{0:T(1024)}, u32[]{:S(2)}) copy-start(f32[1024]{0:T(1024)} %get-tuple-element.25) | copy-start | bytes 12292
  109.2 2.2 %copy-start.11 = (f32[1024]{0:T(1024)S(1)}, f32[1024]{0:T(1024)}, u32[]{:S(2)}) copy-start(f32[1024]{0:T(1024)} %get-tuple-element.26) | copy-start | bytes 12292
  109.2 2.2 %copy-start.1 = (f32[1024,768]{1,0:T(8,128)S(1)}, f32[1024,768]{1,0:T(8,128)}, u32[]{:S(2)}) copy-start(f32[1024,768]{1,0:T(8,128)} %get-tuple-element.29) | copy-start | bytes 9437188
  157.8 3.3 %copy-start.16 = (f32[768]{0:T(1024)S(1)}, f32[768]{0:T(1024)}, u32[]{:S(2)}) copy-start(f32[768]{0:T(1024)} %param.23) | copy-start | bytes 9220
  157.8 3.4 %copy-start.6 = (bf16[1,128,768]{2,1,0:T(8,128)(2,1)S(1)}, bf16[1,128,768]{2,1,0:T(8,128)(2,1)}, u32[]{:S(2)}) copy-start(bf16[1,128,768]{2,1,0:T(8,128)(2,1)} %param.27) | copy-start | bytes 589828

commit v3 on v2

--- a/solution.py
+++ b/solution.py
@@ -28,18 +28,208 @@
     return (jnp.cos(angles), jnp.sin(angles))
 
 
-def rotate(values, cosine_table, sine_table):
+def swap_matrix(size):
+    source = lax.broadcasted_iota(jnp.int32, (size, size), 0)
+    target = lax.broadcasted_iota(jnp.int32, (size, size), 1)
+    dim = lax.rem(target, HD)
     half_rot = ROT // 2
-    lower = values[..., :half_rot]
-    upper = values[..., half_rot : 2 * half_rot]
-    return jnp.concatenate(
-        [
-            lower * cosine_table - upper * sine_table,
-            upper * cosine_table + lower * sine_table,
-            values[..., 2 * half_rot :],
+    minus = (dim < half_rot) & (source == target + half_rot)
+    plus = (dim >= half_rot) & (dim < ROT) & (source == target - half_rot)
+    return jnp.where(plus, 1.0, 0.0) - jnp.where(minus, 1.0, 0.0)
+
+
+def swapped(values, matrix):
+    return lax.dot_general(
+        values,
+        matrix,
+        (((1,), (0,)), ((), ())),
+        preferred_element_type=jnp.float32,
+        precision=lax.Precision.HIGHEST,
+    )
+
+
+def compute_kernel(
+    width,
+    units,
+    share,
+    row,
+    columns,
+    cosines,
+    sines,
+    norms,
+    up_bias,
+    qkv_bias,
+    partial,
+    grads,
+    norm_grads,
+    grad_b_up,
+    grad_b_qkv,
+    xhats,
+    inverses,
+    norm_one,
+    norm_two,
+    queries,
+    keys,
+    values,
+    mixed,
+    grad_attended,
+    grad_pre,
+    grad_query,
+    grad_key,
+    grad_value,
+    grad_projected,
+    hot,
+):
+    f32, bf16 = jnp.float32, jnp.bfloat16
+    length = row.shape[0]
+    tile = math.gcd(length, 256)
+    tiles = length // tile
+    both = units + HD
+    scale = 1.0 / math.sqrt(HD)
+    matrix = swap_matrix(2 * HD)
+    norm_grads[...] = jnp.zeros_like(norm_grads)
+    grad_b_up[...] = jnp.zeros_like(grad_b_up)
+    grad_b_qkv[...] = jnp.zeros_like(grad_b_qkv)
+    grad_key[...] = jnp.zeros_like(grad_key)
+    grad_value[...] = jnp.zeros_like(grad_value)
+
+    def first_pass(step, carry):
+        here = pl.ds(pl.multiple_of(step * tile, tile), tile)
+        tokens = row[here, :width].astype(f32)
+        centered = tokens - jnp.mean(tokens, axis=-1, keepdims=True)
+        variance = jnp.mean(centered * centered, axis=-1, keepdims=True)
+        inverse = lax.rsqrt(variance + NORM_EPSILON)
+        xhat = centered * inverse
+        xhats[here, :] = xhat
+        inverses[here, :] = inverse
+        one = (xhat * norms[0:1, :] + norms[1:2, :]).astype(bf16)
+        two = (xhat * norms[2:3, :] + norms[3:4, :]).astype(bf16)
+        norm_one[here, :] = one
+        norm_two[here, :] = two
+        projected = dot_f32(one, columns[:, both + units :]) + qkv_bias[...]
+        turning = projected[:, : 2 * HD]
+        turned = turning * cosines[here, :] + swapped(turning, matrix) * sines[here, :]
+        queries[here, :] = (turned[:, :HD].astype(bf16).astype(f32) * scale).astype(bf16)
+        keys[here, :] = turned[:, HD:].astype(bf16)
+        values[here, :] = projected[:, 2 * HD :].astype(bf16)
+        lane = lax.broadcasted_iota(jnp.int32, (tile, 128), 1).astype(f32)
+        segment = row[here, 2 * width :].astype(f32)
+        hot[here, :] = jnp.where(segment == lane, 1.0, 0.0).astype(bf16)
+        pre = dot_f32(two, columns[:, both : both + units]) + up_bias[...]
+        cumulative = 0.5 * (1.0 + lax.erf(pre * math.sqrt(0.5)))
+        density = jnp.exp(pre * pre * -0.5) * (1.0 / math.sqrt(2.0 * math.pi))
+        mixed[here, :units] = (pre * cumulative).astype(bf16)
+        grad_mixed = dot_f32(row[here, width : 2 * width], columns[:, :both])
+        slope = (grad_mixed[:, :units] * (cumulative + pre * density)).astype(bf16)
+        grad_pre[here, :] = slope
+        grad_b_up[...] += jnp.sum(slope.astype(f32), axis=0, keepdims=True)
+        grad_attended[here, :] = grad_mixed[:, units:].astype(bf16)
+        return carry
+
+    lax.fori_loop(0, tiles, first_pass, 0)
+
+    for step in range(tiles):
+        here = pl.ds(step * tile, tile)
+        seen = (step + 1) * tile
+        query, key, value = queries[here, :], keys[:seen, :], values[:seen, :]
+        scores = dot_f32(query, key, LAST)
+        same = dot_f32(hot[here, :], hot[:seen, :], LAST) > 0.5
+        at_query = lax.broadcasted_iota(jnp.int32, (tile, seen), 0) + step * tile
+        at_key = lax.broadcasted_iota(jnp.int32, (tile, seen), 1)
+        scores = jnp.where(same & (at_key <= at_query), scores, NEG_LARGE)
+        exponent = jnp.exp(scores - jnp.max(scores, axis=-1, keepdims=True))
+        softmax = exponent / jnp.sum(exponent, axis=-1, keepdims=True)
+        softmax_low = softmax.astype(bf16)
+        attended = dot_f32(softmax_low, value)
+        mixed[here, units:] = attended.astype(bf16)
+        grad_rows = grad_attended[here, :]
+        grad_dots = jnp.sum(grad_rows.astype(f32) * attended, axis=-1, keepdims=True)
+        grad_probs = dot_f32(grad_rows, value, LAST)
+        grad_scores = (softmax * (grad_probs - grad_dots)).astype(bf16)
+        grad_query[here, :] = dot_f32(grad_scores, key) * scale
+        grad_key[:, :seen] += dot_f32(query, grad_scores, ROWS)
+        grad_value[:, :seen] += dot_f32(grad_rows, softmax_low, ROWS)
+
+    for step in range(tiles):
+        here = pl.ds(step * tile, tile)
+        key_rows = grad_key[:, step * tile : (step + 1) * tile].T
+        value_rows = grad_value[:, step * tile : (step + 1) * tile].T
+        turning = jnp.concatenate([grad_query[here, :], key_rows], axis=-1)
+        turned = turning * cosines[here, :] - swapped(turning, matrix) * sines[here, :]
+        pulled = jnp.concatenate([turned, value_rows], axis=-1).astype(bf16)
+        grad_projected[here, :] = pulled
+        grad_b_qkv[...] += jnp.sum(pulled.astype(f32), axis=0, keepdims=True)
+
+    def last_pass(step, carry):
+        here = pl.ds(pl.multiple_of(step * tile, tile), tile)
+        branch = dot_f32(mixed[here, :], columns[:, :both], LAST).astype(bf16)
+        for part in range(width // share):
+            partial[part, here, :share] = branch[:, part * share : (part + 1) * share]
+        xhat = xhats[here, :]
+        grad_one = dot_f32(grad_projected[here, :], columns[:, both + units :], LAST)
+        grad_two = dot_f32(grad_pre[here, :], columns[:, both : both + units], LAST)
+        norm_grads[0:1, :] += jnp.sum(grad_one * xhat, axis=0, keepdims=True)
+        norm_grads[1:2, :] += jnp.sum(grad_one, axis=0, keepdims=True)
+        norm_grads[2:3, :] += jnp.sum(grad_two * xhat, axis=0, keepdims=True)
+        norm_grads[3:4, :] += jnp.sum(grad_two, axis=0, keepdims=True)
+        pulled = grad_one * norms[0:1, :] + grad_two * norms[2:3, :]
+        term = inverses[here, :] * (
+            pulled
+            - jnp.mean(pulled, axis=-1, keepdims=True)
+            - xhat * jnp.mean(pulled * xhat, axis=-1, keepdims=True)
+        )
+        term = term.astype(bf16)
+        for part in range(width // share):
+            partial[part, here, share:] = term[:, part * share : (part + 1) * share]
+        return carry
+
+    lax.fori_loop(0, tiles, last_pass, 0)
+
+    chunk = math.gcd(width, 256)
+    for first in range(0, width, chunk):
+        here = pl.ds(first, chunk)
+        cotangents = row[:, width + first : width + first + chunk]
+        grads[here, :both] = dot_f32(cotangents, mixed[...], ROWS).astype(bf16)
+        up_grads = dot_f32(norm_two[:, here], grad_pre[...], ROWS).astype(bf16)
+        grads[here, both : both + units] = up_grads
+        qkv_grads = dot_f32(norm_one[:, here], grad_projected[...], ROWS).astype(bf16)
+        grads[here, both + units :] = qkv_grads
+
+
+def compute_all(row, columns, cosines, sines, norms, up_bias, qkv_bias, width, units, share):
+    f32, bf16 = jnp.float32, jnp.bfloat16
+    length = row.shape[0]
+    vmem = pl.BlockSpec(memory_space=pltpu.VMEM)
+    return pl.pallas_call(
+        functools.partial(compute_kernel, width, units, share),
+        out_shape=(
+            jax.ShapeDtypeStruct((width // share, length, 2 * share), bf16),
+            jax.ShapeDtypeStruct(columns.shape, bf16),
+            jax.ShapeDtypeStruct((4, width), f32),
+            jax.ShapeDtypeStruct((1, units), f32),
+            jax.ShapeDtypeStruct((1, 3 * HD), f32),
+        ),
+        in_specs=[vmem] * 7,
+        out_specs=(vmem,) * 5,
+        scratch_shapes=[
+            pltpu.VMEM((length, width), f32),
+            pltpu.VMEM((length, 1), f32),
+            pltpu.VMEM((length, width), bf16),
+            pltpu.VMEM((length, width), bf16),
+            pltpu.VMEM((length, HD), bf16),
+            pltpu.VMEM((length, HD), bf16),
+            pltpu.VMEM((length, HD), bf16),
+            pltpu.VMEM((length, units + HD), bf16),
+            pltpu.VMEM((length, HD), bf16),
+            pltpu.VMEM((length, units), bf16),
+            pltpu.VMEM((length, HD), f32),
+            pltpu.VMEM((HD, length), f32),
+            pltpu.VMEM((HD, length), f32),
+            pltpu.VMEM((length, 3 * HD), bf16),
+            pltpu.VMEM((length, 128), bf16),
         ],
-        axis=-1,
-    )
+        compiler_params=pltpu.CompilerParams(vmem_limit_bytes=56 * 2**20),
+    )(row, columns, cosines, sines, norms, up_bias, qkv_bias)
 
 
 MESH = pl.DeviceIdType.MESH
@@ -383,10 +573,10 @@
     out_blocks = jnp.pad(w_out, ((0, 0), (0, pad_heads))).reshape(owned, ctx, head_width)
     blocks = jnp.concatenate(
         [
+            w_down.reshape(owned, ctx, units).transpose(1, 0, 2),
+            out_blocks.transpose(1, 0, 2),
             w_up.reshape(owned, ctx, units).transpose(1, 0, 2),
-            w_down.reshape(owned, ctx, units).transpose(1, 0, 2),
             qkv_blocks.reshape(ctx, owned, 3 * head_width),
-            out_blocks.transpose(1, 0, 2),
         ],
         axis=-1,
     )
@@ -397,130 +587,55 @@
     packed = jnp.concatenate([inputs[0], cotangent[0], seg_columns], axis=-1)
     row, columns = gather_all(packed, blocks, dp, ctx, tp)
     columns = columns[:, :, :owned, :block_width].reshape(width, -1)
-    up = columns[:, :units]
-    down = columns[:, units : 2 * units]
-    qkv = columns[:, 2 * units : 2 * units + 3 * head_width]
-    out = columns[:, 2 * units + 3 * head_width :]
-
-    tokens = row[:, :width].astype(f32)
-    grad_out = row[:, width : 2 * width]
-    seg = row[:, 2 * width]
-
     qkv_bias = jnp.pad(b_qkv, ((0, 0), (0, pad_heads))).reshape(3, ctx, head_width)
     qkv_bias = lax.dynamic_index_in_dim(qkv_bias, my_ctx, 1, keepdims=False).reshape(-1)
     up_bias = lax.dynamic_slice_in_dim(b_up, my_ctx * units, units, 0)
 
-    average = jnp.mean(tokens, axis=-1, keepdims=True)
-    centered = tokens - average
-    inverse = lax.rsqrt(jnp.mean(centered * centered, axis=-1, keepdims=True) + NORM_EPSILON)
-    xhat = centered * inverse
-    norm_one = (xhat * gain_one + bias_one).astype(bf16)
-    norm_two = (xhat * gain_two + bias_two).astype(bf16)
-
-    projected = dot_f32(norm_one, qkv) + qkv_bias
     cosine_table, sine_table = angle_tables(0, length)
-    softmax_scale = 1.0 / math.sqrt(HD)
-    position = jnp.arange(length)
-    allowed = (position[None, :] <= position[:, None]) & (seg[None, :] == seg[:, None])
-    kept = []
-    for slot in range(slots):
-        first = slot * HD
-        query = rotate(projected[:, first : first + HD], cosine_table, sine_table).astype(bf16)
-        first += head_width
-        key = rotate(projected[:, first : first + HD], cosine_table, sine_table).astype(bf16)
-        first += head_width
-        value = projected[:, first : first + HD].astype(bf16)
-        scores = jnp.where(allowed, dot_f32(query, key, LAST) * softmax_scale, NEG_LARGE)
-        exponent = jnp.exp(scores - jnp.max(scores, axis=-1, keepdims=True))
-        softmax = exponent / jnp.sum(exponent, axis=-1, keepdims=True)
-        attended = dot_f32(softmax.astype(bf16), value)
-        kept.append((query, key, value, softmax, attended))
-    attended_low = jnp.concatenate([item[4] for item in kept], axis=-1).astype(bf16)
-
-    pre_gelu = dot_f32(norm_two, up) + up_bias
-    activated = jax.nn.gelu(pre_gelu, approximate=False).astype(bf16)
-    branch = dot_f32(attended_low, out, LAST) + dot_f32(activated, down, LAST)
-
-    grad_attended = dot_f32(grad_out, out).astype(bf16)
-    grad_activated = dot_f32(grad_out, down)
-    gelu_pull = jax.vjp(lambda current: jax.nn.gelu(current, approximate=False), pre_gelu)[1]
-    grad_pre = gelu_pull(grad_activated)[0].astype(bf16)
-    grad_w_out = dot_f32(grad_out, attended_low, ROWS)
-    grad_w_down = dot_f32(grad_out, activated, ROWS)
-    grad_w_up = dot_f32(norm_two, grad_pre, ROWS)
-    grad_b_up = jnp.sum(grad_pre.astype(f32), axis=0)
-    grad_norm_two = dot_f32(grad_pre, up, LAST)
-
-    pieces = ([], [], [])
-    for slot, (query, key, value, softmax, attended) in enumerate(kept):
-        grad_rows = grad_attended[:, slot * HD : (slot + 1) * HD]
-        grad_dots = jnp.sum(grad_rows.astype(f32) * attended, axis=-1, keepdims=True)
-        grad_probs = dot_f32(grad_rows, value, LAST)
-        grad_scores = (softmax * (grad_probs - grad_dots)).astype(bf16)
-        grad_query = dot_f32(grad_scores, key) * softmax_scale
-        grad_key = dot_f32(grad_scores, query, ROWS) * softmax_scale
-        pieces[0].append(rotate(grad_query, cosine_table, -sine_table))
-        pieces[1].append(rotate(grad_key, cosine_table, -sine_table))
-        pieces[2].append(dot_f32(softmax.astype(bf16), grad_rows, ROWS))
-    grad_projected = jnp.concatenate(pieces[0] + pieces[1] + pieces[2], axis=-1).astype(bf16)
-    grad_w_qkv = dot_f32(norm_one, grad_projected, ROWS)
-    grad_b_qkv = jnp.sum(grad_projected.astype(f32), axis=0)
-    grad_norm_one = dot_f32(grad_projected, qkv, LAST)
-
-    grad_gain_one = jnp.sum(grad_norm_one * xhat, axis=0)
-    grad_bias_one = jnp.sum(grad_norm_one, axis=0)
-    grad_gain_two = jnp.sum(grad_norm_two * xhat, axis=0)
-    grad_bias_two = jnp.sum(grad_norm_two, axis=0)
-    pulled = grad_norm_one * gain_one + grad_norm_two * gain_two
-    input_term = inverse * (
-        pulled
-        - jnp.mean(pulled, axis=-1, keepdims=True)
-        - xhat * jnp.mean(pulled * xhat, axis=-1, keepdims=True)
+    rest = jnp.zeros((length, HD - ROT), f32)
+    cosines = jnp.concatenate([cosine_table, cosine_table, rest + 1.0], axis=-1)
+    sines = jnp.concatenate([sine_table, sine_table, rest], axis=-1)
+    norms = jnp.stack([gain_one, bias_one, gain_two, bias_two])
+    partial, grads, norm_grads, grad_b_up, grad_b_qkv = compute_all(
+        row,
+        columns,
+        jnp.concatenate([cosines, cosines], axis=-1),
+        jnp.concatenate([sines, sines], axis=-1),
+        norms,
+        up_bias[None],
+        qkv_bias[None],
+        width,
+        units,
+        share,
     )
 
-    grads = jnp.concatenate([grad_w_up, grad_w_down, grad_w_qkv, grad_w_out], axis=-1)
-    grads = grads.astype(bf16).reshape(dp, ctx, owned, -1)
+    grads = grads.reshape(dp, ctx, owned, -1)
     grads = jnp.pad(grads, ((0, 0), (0, 0), (0, pad_rows), (0, pad_width)))
 
     grad_bias = jnp.sum(cotangent[0].astype(f32), axis=0) * (my_tp == 0).astype(f32)
     place = (jnp.arange(tp)[:, None] == my_tp) & (jnp.arange(ctx)[None, :] == my_ctx)
-    local = jnp.concatenate([grad_b_qkv, grad_b_up])
+    local = jnp.concatenate([grad_b_qkv[0], grad_b_up[0]])
     spread = jnp.where(place[:, :, None], local, 0.0)
     vectors = jnp.concatenate(
         [
-            grad_gain_one,
-            grad_bias_one,
-            grad_gain_two,
-            grad_bias_two,
+            norm_grads.reshape(-1),
             grad_bias,
             spread.reshape(-1),
         ]
     )
     vector_size = vectors.shape[0]
     vectors = jnp.pad(vectors, (0, -vector_size % 1024)).reshape(-1, 128)
-    branch_low, input_low = branch.astype(bf16), input_term.astype(bf16)
-    partial = jnp.stack(
-        [
-            jnp.concatenate(
-                [
-                    branch_low[:, part * share : (part + 1) * share],
-                    input_low[:, part * share : (part + 1) * share],
-                ],
-                axis=-1,
-            )
-            for part in range(tp)
-        ]
-    )
     sums, own, total = reduce_all(partial, grads, vectors, dp, ctx, tp)
     branch_share, input_share = sums[:, :share], sums[:, share:]
     own = own[:, :owned, :block_width].astype(f32)
-    own_up = own[:, :, :units].transpose(1, 0, 2).reshape(owned, -1)
-    own_down = own[:, :, units : 2 * units].transpose(1, 0, 2).reshape(owned, -1)
-    own_qkv = own[:, :, 2 * units : 2 * units + 3 * head_width]
-    own_qkv = own_qkv.reshape(ctx, owned, 3, head_width).transpose(1, 2, 0, 3)
-    own_qkv = own_qkv.reshape(owned, 3, ctx * head_width)[:, :, : heads * HD]
-    own_out = own[:, :, 2 * units + 3 * head_width :].transpose(1, 0, 2)
+    own_down = own[:, :, :units].transpose(1, 0, 2).reshape(owned, -1)
+    own_out = own[:, :, units : units + head_width].transpose(1, 0, 2)
     own_out = own_out.reshape(owned, -1)[:, : heads * HD]
+    first = units + head_width
+    own_up = own[:, :, first : first + units].transpose(1, 0, 2).reshape(owned, -1)
+    own_qkv = own[:, :, first + units :].reshape(ctx, owned, 3, head_width)
+    own_qkv = own_qkv.transpose(1, 2, 0, 3).reshape(owned, 3, ctx * head_width)
+    own_qkv = own_qkv[:, :, : heads * HD]
     total = total.reshape(-1)[:vector_size]
     spread = total[5 * width :].reshape(tp, ctx, -1)
     spread = lax.dynamic_index_in_dim(spread, my_tp, 0, keepdims=False)

time: 167 us -> 133 us (0.80)
  matrix products: 30.9 us -> 0 us
  Pallas kernels: 84.5 us -> 103 us
  other arithmetic: 21.3 us -> 6.17 us
  local copies, waits for them, and re-layouts: 27 us -> 21.5 us
    dot_general x18 -> x0, matrix products: 30.9 us -> none  [dot_f32(): return lax.dot_general(a, b, dims, preferred_element_type=jnp.float32)]
    pallas_call x0 -> x1, Pallas kernels: none -> 18.8 us  [compute_all(): pl.pallas_call(functools.partial(compute_kernel, width, units, share), ou...]
    reduce_sum x5 -> x0, other arithmetic: 11.2 us -> none  [the longest x1 5.77 us: on_device(): grad_gain_two = jnp.sum(grad_norm_two * xhat, axis=0)]
    dot_general x2 -> x0, local copies, waits for them, and re-layouts: 7.32 us -> none  [dot_f32(): return lax.dot_general(a, b, dims, preferred_element_type=jnp.float32)]
    another operation x4 -> x5, local copies, waits for them, and re-layouts: 6.45 us -> 0.66 us  [the longest x1 0.65 us: on_device(): qkv_bias[None]]
    concatenate x1 -> x2, local copies, waits for them, and re-layouts: 0.01 us -> 3.69 us  [the longest x1 1.95 us: on_device(): jnp.concatenate([cosines, cosines], axis=-1)]
    unnamed x46 -> x22, local copies, waits for them, and re-layouts: 0.63 us -> 3.13 us
    convert_element_type x2 -> x0, other arithmetic: 1.97 us -> none  [the longest x1 1.27 us: on_device(): branch_low, input_low = (branch.astype(bf16), input_term.astype(bf16))]
where the time goes in v3:
time: 133 us; the launch traced here: 132 us
  Pallas kernels  103 us (77%)
  local copies, waits for them, and re-layouts  21.5 us (16%)
  other arithmetic  6.17 us (5%)
    pallas_call x1, Pallas kernels, reduce_all(): pl.pallas_call(functools.partial(reduce_kernel, ctx, dp, tp), out_shape=(...  42.7 us
    pallas_call x1, Pallas kernels, gather_all(): pl.pallas_call(functools.partial(gather_kernel, ctx, dp, tp), out_shape=(...  41.7 us
    pallas_call x1, Pallas kernels, compute_all(): pl.pallas_call(functools.partial(compute_kernel, width, units, share), ou...  18.8 us
    unnamed x22, local copies, waits for them, and re-layouts  3.13 us

profile of v3, /device:TPU:0, one launch (start us, length us, event | category | flops | bytes accessed | tf_op | source)
XLA Modules:
  0.0 131.9 jit_solution(3329099606424575616)
XLA Ops:
  0.6 0.0 copy-start.4
  0.7 0.0 copy-start.10
  0.7 0.0 copy-start.3
  0.7 0.0 copy-start.2
  0.7 1.4 %dynamic_slice.21 = f32[192]{0:T(256)} dynamic-slice(f32[1536]{0:T(1024)} %param.25, s32[]{:T(128)S(6)} %select_n.25), dynamic_slice_sizes={192} | dynamic-slice | bytes 1540 | tf_op jit(solution)/shard_map/dynamic_slice | solution.py:592
  2.1 0.7 pad.18
  2.8 0.1 reshape.165
  2.9 0.6 broadcast_in_dim_reshape.3.qkv_bias
  3.5 1.1 reshape.159
  4.7 1.1 reshape.161
  5.8 0.1 copy_bitcast_fusion.1
  5.9 0.9 pad.17
  6.8 0.2 reshape.162
  7.0 0.3 copy.64
  7.2 0.2 reshape.163
  7.5 0.1 reshape.160
  7.6 1.0 pad_maximum_fusion.blocks
  8.6 0.1 broadcast_in_dim.40
  8.7 0.0 copy-done.3
  8.7 0.0 copy-done.2
  8.8 0.8 pad_maximum_fusion.1.packed
  9.6 41.7 %shard_map.237 = (bf16[1024,1664]{1,0:T(8,128)(2,1)}, bf16[2,8,48,640]{3,2,1,0:T(8,128)(2,1)}) custom-call(bf16[128,1664]{1,0:T(8,128)(2,1)} %pad_maximum_fusion.1.packed, bf16[8,48,640]{2,1,0:T(8,128)(2,1)} %pad_maximum_fusion.blocks), custom_call_target="tpu_custom_call" | custom-call | tf_op jit(solution)/shard_map/pallas_call | solution.py:346
  51.3 1.9 %multiply_sine_fusion = (f32[1024,8]{1,0:T(8,128)S(1)}, f32[1024,8]{1,0:T(8,128)S(1)}) fusion(f32[1024]{0:T(1024)S(1)} %iota_convert_fusion, f32[8]{0:T(128)S(1)} %negate_power_fusion), kind=kLoop, calls=%fused_computation | loop fusion | flops 8192 | bytes 69664 | tf_op jit(solution)/shard_map/sin | solution.py:28
  53.2 0.0 copy-start.5
  53.3 0.0 copy-start.6
  53.3 0.0 copy-start.7
  53.3 0.0 copy-start.8
  53.3 2.0 %concatenate.24.cosines = f32[1024,128]{1,0:T(8,128)} concatenate(f32[1024,8]{1,0:T(8,128)S(1)} %get-tuple-element.45, f32[1024,8]{1,0:T(8,128)S(1)} %get-tuple-element.45, f32[1024,48]{1,0:T(8,128)S(1)} %add.42, f32[1024,8]{1,0:T(8,128)S(1)} %get-tuple-element.45, f32[1024,8]{1,0:T(8,128)S(1)} %get-tuple-element.45, f32[1024,48]{1,0:T(8,128)S(1)} %add.42), dimensions={1} | concatenate | bytes 1048576 | tf_op jit(solution)/shard_map/concatenate | solution.py:602
  55.3 1.7 %concatenate.25.sines = f32[1024,128]{1,0:T(8,128)} concatenate(f32[1024,8]{1,0:T(8,128)S(1)} %get-tuple-element.44, f32[1024,8]{1,0:T(8,128)S(1)} %get-tuple-element.44, f32[1024,48]{1,0:T(8,128)S(1)} %broadcast_in_dim.41, f32[1024,8]{1,0:T(8,128)S(1)} %get-tuple-element.44, f32[1024,8]{1,0:T(8,128)S(1)} %get-tuple-element.44, f32[1024,48]{1,0:T(8,128)S(1)} %broadcast_in_dim.41), dimensions={1} | concatenate | bytes 1048576 | tf_op jit(solution)/shard_map/concatenate | solution.py:603
  57.0 0.0 copy-done.5
  57.1 0.6 pad_maximum_fusion.2.norms
  57.7 18.8 %shard_map.238 = (bf16[2,1024,768]{2,1,0:T(8,128)(2,1)}, bf16[768,640]{1,0:T(8,128)(2,1)}, f32[4,768]{1,0:T(4,128)}, f32[1,192]{1,0:T(1,128)}, f32[1,192]{1,0:T(1,128)}) custom-call(bf16[1024,1664]{1,0:T(8,128)(2,1)} %get-tuple-element.23.row, bf16[768,640]{1,0:T(8,128)(2,1)} %bitcast.62, f32[1024,128]{1,0:T(8,128)} %concatenate.24.cosines, ...), custom_call_target="tpu_custom_call" | custom-call | tf_op jit(solution)/shard_map/pallas_call | solution.py:203
  76.5 0.8 pad_maximum_fusion.3
  77.3 0.1 broadcast_and_fusion
  77.3 0.1 broadcast_select_fusion
  77.4 0.7 reshape.167
  78.2 0.0 copy-start
  78.2 1.9 %copy-done = bf16[2,1024,768]{2,1,0:T(8,128)(2,1)S(1)} copy-done((bf16[2,1024,768]{2,1,0:T(8,128)(2,1)S(1)}, bf16[2,1024,768]{2,1,0:T(8,128)(2,1)}, u32[]{:S(2)}) %copy-start) | copy-done | bytes 3145752
  80.1 1.2 copy-done.1
  81.3 42.7 %shard_map.239 = (f32[128,768]{1,0:T(8,128)S(1)}, bf16[8,48,640]{2,1,0:T(8,128)(2,1)S(1)}, f32[80,128]{1,0:T(8,128)S(1)}) custom-call(bf16[2,1024,768]{2,1,0:T(8,128)(2,1)S(1)} %copy-done, bf16[2,8,48,640]{3,2,1,0:T(8,128)(2,1)S(1)} %bitcast.58, f32[80,128]{1,0:T(8,128)S(1)} %fusion.3.vectors), custom_call_target="tpu_custom_call" | custom-call | tf_op jit(solution)/shard_map/pallas_call | solution.py:510
  124.0 0.1 convert_element_type.91
  124.1 0.1 slice_bitcast_fusion
  124.1 0.2 copy.57
  124.4 0.9 reshape.175
  125.2 0.2 copy.58
  125.5 0.0 copy-start.9
  125.5 0.9 reshape.177
  126.3 0.1 slice.97
  126.5 0.2 reshape.169
  126.7 0.3 copy.54
  127.1 0.2 reshape.170
  127.2 0.7 slice.98
  127.9 0.1 slice_bitcast_fusion.2
  128.1 0.1 copy.56
  128.1 0.1 reshape.174
  128.2 0.6 slice.102
  128.9 0.1 dynamic_slice.23
  128.9 0.8 fusion
  129.8 0.1 fusion.4
  129.8 0.1 reshape.172
  129.9 0.1 reshape.173
  130.0 0.6 slice.100
  130.6 0.7 reshape.176
  131.3 0.6 slice_bitcast_fusion.3
  (29 shorter events, 0.3 us)
Async XLA Ops:
  0.6 6.8 %copy-start.4 = (bf16[48,384]{1,0:T(8,128)(2,1)S(1)}, bf16[48,384]{1,0:T(8,128)(2,1)}, u32[]{:S(2)}) copy-start(bf16[48,384]{1,0:T(8,128)(2,1)} %param.22) | copy-start | bytes 110596
  0.7 8.0 %copy-start.10 = (s32[1,128]{1,0:T(1,128)S(1)}, s32[1,128]{1,0:T(1,128)}, u32[]{:S(2)}) copy-start(s32[1,128]{1,0:T(1,128)} %param.15) | copy-start | bytes 1540
  0.7 8.1 %copy-start.3 = (bf16[1,128,768]{2,1,0:T(8,128)(2,1)S(1)}, bf16[1,128,768]{2,1,0:T(8,128)(2,1)}, u32[]{:S(2)}) copy-start(bf16[1,128,768]{2,1,0:T(8,128)(2,1)} %param.14) | copy-start | bytes 589828
  0.7 8.1 %copy-start.2 = (bf16[1,128,768]{2,1,0:T(8,128)(2,1)S(1)}, bf16[1,128,768]{2,1,0:T(8,128)(2,1)}, u32[]{:S(2)}) copy-start(bf16[1,128,768]{2,1,0:T(8,128)(2,1)} %param.27) | copy-start | bytes 589828
  53.2 3.8 %copy-start.5 = (f32[768]{0:T(1024)S(1)}, f32[768]{0:T(1024)}, u32[]{:S(2)}) copy-start(f32[768]{0:T(1024)} %param.16) | copy-start | bytes 9220
  53.3 3.8 %copy-start.6 = (f32[768]{0:T(1024)S(1)}, f32[768]{0:T(1024)}, u32[]{:S(2)}) copy-start(f32[768]{0:T(1024)} %param.17) | copy-start | bytes 9220
  53.3 3.8 %copy-start.7 = (f32[768]{0:T(1024)S(1)}, f32[768]{0:T(1024)}, u32[]{:S(2)}) copy-start(f32[768]{0:T(1024)} %param.18) | copy-start | bytes 9220
  53.3 3.8 %copy-start.8 = (f32[768]{0:T(1024)S(1)}, f32[768]{0:T(1024)}, u32[]{:S(2)}) copy-start(f32[768]{0:T(1024)} %param.19) | copy-start | bytes 9220
  78.2 1.9 %copy-start = (bf16[2,1024,768]{2,1,0:T(8,128)(2,1)S(1)}, bf16[2,1024,768]{2,1,0:T(8,128)(2,1)}, u32[]{:S(2)}) copy-start(bf16[2,1024,768]{2,1,0:T(8,128)(2,1)} %get-tuple-element.25.partial) | copy-start | bytes 9437188
  80.1 1.2 copy-start.1
  125.5 3.4 %copy-start.9 = (f32[768]{0:T(1024)S(1)}, f32[768]{0:T(1024)}, u32[]{:S(2)}) copy-start(f32[768]{0:T(1024)} %param.23) | copy-start | bytes 9220

commit v4 on v3

--- a/solution.py
+++ b/solution.py
@@ -6,6 +6,7 @@
 from jax import lax
 from jax.experimental import pallas as pl
 from jax.experimental.pallas import tpu as pltpu
+import numpy as np
 from jax.sharding import PartitionSpec as P
 
 HD = 64
@@ -21,11 +22,14 @@
     return lax.dot_general(a, b, dims, preferred_element_type=jnp.float32)
 
 
-def angle_tables(first_row, length):
-    positions = (first_row + jnp.arange(length)).astype(jnp.float32)
-    frequency = 10000.0 ** (-(jnp.arange(ROT // 2).astype(jnp.float32) * 2.0 / ROT))
-    angles = positions[:, None] * frequency[None, :]
-    return (jnp.cos(angles), jnp.sin(angles))
+def angle_tables(length):
+    frequency = np.float32(10000.0) ** (-(np.arange(ROT // 2, dtype=np.float32) * 2.0 / ROT))
+    angles = np.arange(length, dtype=np.float32)[:, None] * frequency.astype(np.float32)
+    rest = np.zeros((length, HD - ROT))
+    angles = angles.astype(np.float64)
+    cosines = np.concatenate([np.cos(angles), np.cos(angles), rest + 1.0], axis=-1)
+    sines = np.concatenate([np.sin(angles), np.sin(angles), rest], axis=-1)
+    return tuple(np.concatenate([t, t], axis=-1).astype(np.float32) for t in (cosines, sines))
 
 
 def swap_matrix(size):
@@ -48,10 +52,120 @@
     )
 
 
+class Tree:
+    def __init__(self, copies, place, partial, from_core, to_x, from_x, to_z, from_z):
+        self.copies, self.place, self.partial, self.from_core = copies, place, partial, from_core
+        self.to_x, self.from_x, self.to_z, self.from_z = to_x, from_x, to_z, from_z
+        self.over_core, self.over_x, self.over_z = {}, {}, {}
+
+    def send_core(self, step):
+        here = self.place.group(step)
+        self.over_core[step] = self.copies.start(
+            self.partial.at[1 - self.place.tp, here], self.from_core.at[here], self.place.sibling
+        )
+
+    def local_sum(self, step, x):
+        here = self.place.token_rows(step, x)
+        mine = self.partial[self.place.tp, here, :].astype(jnp.float32)
+        return mine + self.from_core[here, :].astype(jnp.float32)
+
+    def send_x(self, step):
+        self.over_core[step].wait_recv()
+        self.to_x[step] = self.local_sum(step, INNER - 1 - self.place.x).astype(jnp.bfloat16)
+        self.over_x[step] = self.copies.start(
+            self.to_x.at[step], self.from_x.at[step], self.place.partner
+        )
+
+    def x_sum(self, step):
+        self.over_x[step].wait_recv()
+        local = self.local_sum(step, self.place.x)
+        return local + self.from_x[step].astype(jnp.float32)
+
+    def send_z(self, step):
+        self.to_z[step - 1] = self.x_sum(step).astype(jnp.bfloat16)
+        self.over_z[step] = self.copies.start(
+            self.to_z.at[step - 1], self.from_z.at[step - 1], self.place.along(step)
+        )
+
+    def result(self):
+        total = self.x_sum(0)
+        for step in range(1, self.place.outer):
+            self.over_z[step].wait_recv()
+            total = total + self.from_z[step - 1].astype(jnp.float32)
+        return total
+
+
+class Place:
+    def __init__(self, ctx, dp, tp, rows):
+        self.outer, self.rows = ctx // INNER, rows
+        self.ctx, self.dp, self.tp = (lax.axis_index(name) for name in ("ctx", "dp", "tp"))
+        self.z, self.x = self.ctx // INNER, lax.rem(self.ctx, INNER)
+        self.partner = {"ctx": self.z * INNER + (INNER - 1 - self.x)}
+        self.sibling = {"tp": tp - 1 - self.tp}
+
+    def along(self, step):
+        return {"ctx": lax.rem(self.z + step, self.outer) * INNER + self.x}
+
+    def group(self, step):
+        first = lax.rem(self.z + step, self.outer) * INNER * self.rows
+        return pl.ds(pl.multiple_of(first, INNER * self.rows), INNER * self.rows)
+
+    def token_rows(self, step, x):
+        first = (lax.rem(self.z + step, self.outer) * INNER + x) * self.rows
+        return pl.ds(pl.multiple_of(first, self.rows), self.rows)
+
+
+class Exchange:
+    def __init__(self, copies, place, ctx, dp, grads, from_y, summed, own_grads, local_sem):
+        self.copies, self.place, self.ctx, self.dp = copies, place, ctx, dp
+        self.grads, self.from_y, self.summed = grads, from_y, summed
+        self.own_grads, self.local_sem = own_grads, local_sem
+
+    def send_y(self):
+        self.over_y = []
+        for other in range(1, self.dp):
+            target = lax.rem(self.place.dp + other, self.dp)
+            self.over_y.append(
+                self.copies.start(
+                    self.grads.at[target], self.from_y.at[other - 1], {"dp": target}
+                )
+            )
+
+    def send_ctx(self):
+        for copy in self.over_y:
+            copy.wait_recv()
+        self.over_ctx = []
+        for step in list(range(1, self.ctx)) + [0]:
+            target = lax.rem(self.place.ctx + step, self.ctx)
+            total = self.grads[self.place.dp, target].astype(jnp.float32)
+            for other in range(1, self.dp):
+                total = total + self.from_y[other - 1, target].astype(jnp.float32)
+            self.summed[step] = total.astype(jnp.bfloat16)
+            if step > 0:
+                self.over_ctx.append(
+                    self.copies.start(
+                        self.summed.at[step], self.own_grads.at[self.place.ctx], {"ctx": target}
+                    )
+                )
+        self.own = pltpu.make_async_copy(
+            self.summed.at[0], self.own_grads.at[self.place.ctx], self.local_sem
+        )
+        self.own.start()
+
+    def finish(self):
+        for copy in self.over_ctx:
+            copy.wait_recv()
+        self.own.wait()
+
+
 def compute_kernel(
     width,
     units,
     share,
+    ctx,
+    dp,
+    tp,
+    owned,
     row,
     columns,
     cosines,
@@ -59,12 +173,13 @@
     norms,
     up_bias,
     qkv_bias,
-    partial,
-    grads,
+    sums,
+    early_own,
+    late_own,
+    totals,
     norm_grads,
-    grad_b_up,
-    grad_b_qkv,
-    xhats,
+    local_vector,
+    averages,
     inverses,
     norm_one,
     norm_two,
@@ -79,28 +194,70 @@
     grad_value,
     grad_projected,
     hot,
+    out_partial,
+    out_core,
+    out_to_x,
+    out_from_x,
+    out_to_z,
+    out_from_z,
+    in_partial,
+    in_core,
+    in_to_x,
+    in_from_x,
+    in_to_z,
+    in_from_z,
+    early_grads,
+    early_y,
+    early_sum,
+    late_grads,
+    late_y,
+    late_sum,
+    vectors,
+    core_vector,
+    x_vector,
+    passed_vector,
+    z_vectors,
+    y_vectors,
+    send_sems,
+    recv_sems,
+    local_sems,
 ):
     f32, bf16 = jnp.float32, jnp.bfloat16
     length = row.shape[0]
-    tile = math.gcd(length, 256)
+    rows = length // ctx
+    place = Place(ctx, dp, tp, rows)
+    greet(ctx, dp, tp, place.ctx, place.dp, place.tp)
+    copies = Copies(send_sems, recv_sems)
+    out_tree = Tree(
+        copies, place, out_partial, out_core, out_to_x, out_from_x, out_to_z, out_from_z
+    )
+    in_tree = Tree(copies, place, in_partial, in_core, in_to_x, in_from_x, in_to_z, in_from_z)
+    early = Exchange(
+        copies, place, ctx, dp, early_grads, early_y, early_sum, early_own, local_sems.at[0]
+    )
+    late = Exchange(
+        copies, place, ctx, dp, late_grads, late_y, late_sum, late_own, local_sems.at[1]
+    )
+    order = list(range(1, place.outer)) + [0]
+    tile = INNER * rows
     tiles = length // tile
     both = units + HD
     scale = 1.0 / math.sqrt(HD)
     matrix = swap_matrix(2 * HD)
     norm_grads[...] = jnp.zeros_like(norm_grads)
-    grad_b_up[...] = jnp.zeros_like(grad_b_up)
-    grad_b_qkv[...] = jnp.zeros_like(grad_b_qkv)
+    local_vector[...] = jnp.zeros_like(local_vector)
     grad_key[...] = jnp.zeros_like(grad_key)
     grad_value[...] = jnp.zeros_like(grad_value)
 
     def first_pass(step, carry):
         here = pl.ds(pl.multiple_of(step * tile, tile), tile)
         tokens = row[here, :width].astype(f32)
-        centered = tokens - jnp.mean(tokens, axis=-1, keepdims=True)
+        average = jnp.mean(tokens, axis=-1, keepdims=True)
+        centered = tokens - average
         variance = jnp.mean(centered * centered, axis=-1, keepdims=True)
         inverse = lax.rsqrt(variance + NORM_EPSILON)
         xhat = centered * inverse
-        xhats[here, :] = xhat
+        averages[here, :] = average
         inverses[here, :] = inverse
         one = (xhat * norms[0:1, :] + norms[1:2, :]).astype(bf16)
         two = (xhat * norms[2:3, :] + norms[3:4, :]).astype(bf16)
@@ -122,11 +279,25 @@
         grad_mixed = dot_f32(row[here, width : 2 * width], columns[:, :both])
         slope = (grad_mixed[:, :units] * (cumulative + pre * density)).astype(bf16)
         grad_pre[here, :] = slope
-        grad_b_up[...] += jnp.sum(slope.astype(f32), axis=0, keepdims=True)
+        local_vector[:, 3 * HD : 3 * HD + units] += jnp.sum(slope.astype(f32), axis=0, keepdims=True)
         grad_attended[here, :] = grad_mixed[:, units:].astype(bf16)
         return carry
 
     lax.fori_loop(0, tiles, first_pass, 0)
+
+    def weight_grads(store, first, left, left_first, right):
+        block = ctx * owned
+        for half in range(dp):
+            rows_here = left[:, left_first + half * block : left_first + (half + 1) * block]
+            grad = dot_f32(rows_here, right, ROWS)
+            for owner in range(ctx):
+                store[half, owner, :owned, first : first + right.shape[1]] = grad[
+                    owner * owned : (owner + 1) * owned
+                ].astype(bf16)
+
+    weight_grads(early_grads, 0, row, width, mixed[:, :units])
+    weight_grads(early_grads, units, norm_two, 0, grad_pre[...])
+    early.send_y()
 
     for step in range(tiles):
         here = pl.ds(step * tile, tile)
@@ -149,6 +320,15 @@
         grad_query[here, :] = dot_f32(grad_scores, key) * scale
         grad_key[:, :seen] += dot_f32(query, grad_scores, ROWS)
         grad_value[:, :seen] += dot_f32(grad_rows, softmax_low, ROWS)
+        if step == min(1, tiles - 1):
+            early.send_ctx()
+
+    for step in order:
+        here = place.group(step)
+        branch = dot_f32(mixed[here, :], columns[:, :both], LAST).astype(bf16)
+        for part in range(tp):
+            out_partial[part, here, :] = branch[:, part * share : (part + 1) * share]
+        out_tree.send_core(step)
 
     for step in range(tiles):
         here = pl.ds(step * tile, tile)
@@ -158,14 +338,16 @@
         turned = turning * cosines[here, :] - swapped(turning, matrix) * sines[here, :]
         pulled = jnp.concatenate([turned, value_rows], axis=-1).astype(bf16)
         grad_projected[here, :] = pulled
-        grad_b_qkv[...] += jnp.sum(pulled.astype(f32), axis=0, keepdims=True)
-
-    def last_pass(step, carry):
-        here = pl.ds(pl.multiple_of(step * tile, tile), tile)
-        branch = dot_f32(mixed[here, :], columns[:, :both], LAST).astype(bf16)
-        for part in range(width // share):
-            partial[part, here, :share] = branch[:, part * share : (part + 1) * share]
-        xhat = xhats[here, :]
+        local_vector[:, : 3 * HD] += jnp.sum(pulled.astype(f32), axis=0, keepdims=True)
+
+    weight_grads(late_grads, 0, row, width, mixed[:, units:])
+    weight_grads(late_grads, HD, norm_one, 0, grad_projected[...])
+    late.send_y()
+
+    for step in order:
+        out_tree.send_x(step)
+        here = place.group(step)
+        xhat = (row[here, :width].astype(f32) - averages[here, :]) * inverses[here, :]
         grad_one = dot_f32(grad_projected[here, :], columns[:, both + units :], LAST)
         grad_two = dot_f32(grad_pre[here, :], columns[:, both : both + units], LAST)
         norm_grads[0:1, :] += jnp.sum(grad_one * xhat, axis=0, keepdims=True)
@@ -179,40 +361,119 @@
             - xhat * jnp.mean(pulled * xhat, axis=-1, keepdims=True)
         )
         term = term.astype(bf16)
-        for part in range(width // share):
-            partial[part, here, share:] = term[:, part * share : (part + 1) * share]
-        return carry
-
-    lax.fori_loop(0, tiles, last_pass, 0)
-
-    chunk = math.gcd(width, 256)
-    for first in range(0, width, chunk):
-        here = pl.ds(first, chunk)
-        cotangents = row[:, width + first : width + first + chunk]
-        grads[here, :both] = dot_f32(cotangents, mixed[...], ROWS).astype(bf16)
-        up_grads = dot_f32(norm_two[:, here], grad_pre[...], ROWS).astype(bf16)
-        grads[here, both : both + units] = up_grads
-        qkv_grads = dot_f32(norm_one[:, here], grad_projected[...], ROWS).astype(bf16)
-        grads[here, both + units :] = qkv_grads
-
-
-def compute_all(row, columns, cosines, sines, norms, up_bias, qkv_bias, width, units, share):
+        for part in range(tp):
+            in_partial[part, here, :] = term[:, part * share : (part + 1) * share]
+        in_tree.send_core(step)
+
+    for step in order:
+        in_tree.send_x(step)
+        if step > 0:
+            out_tree.send_z(step)
+
+    own_rows = row[place.token_rows(0, place.x), width : 2 * width].astype(f32)
+    out_bias_grad = jnp.sum(own_rows, axis=0, keepdims=True)
+    out_bias_grad = jnp.where(place.tp == 0, out_bias_grad, 0.0)
+    vectors[...] = jnp.zeros_like(vectors)
+    lines = width // 128
+    for line in range(lines):
+        lanes = slice(line * 128, (line + 1) * 128)
+        for item in range(4):
+            vectors[item * lines + line : item * lines + line + 1, :] = norm_grads[
+                item : item + 1, lanes
+            ]
+        vectors[4 * lines + line : 4 * lines + line + 1, :] = out_bias_grad[:, lanes]
+    slot_lines = local_vector.shape[1] // 128
+    first_line = 5 * lines + (place.tp * ctx + place.ctx) * slot_lines
+    for line in range(slot_lines):
+        vectors[pl.ds(first_line + line, 1), :] = local_vector[:, line * 128 : (line + 1) * 128]
+    vector_core = copies.start(vectors, core_vector, place.sibling)
+
+    late.send_ctx()
+    vector_core.wait_recv()
+    passed_vector[0] = vectors[...] + core_vector[...]
+    vector_x = copies.start(passed_vector.at[0], x_vector, place.partner)
+    for step in range(1, place.outer):
+        in_tree.send_z(step)
+    vector_x.wait_recv()
+    passed_vector[1] = passed_vector[0] + x_vector[...]
+    z_vectors[place.z] = passed_vector[1]
+    vector_z = [
+        copies.start(passed_vector.at[1], z_vectors.at[place.z], place.along(step))
+        for step in range(1, place.outer)
+    ]
+    sums[:, :share] = out_tree.result()
+    for copy in vector_z:
+        copy.wait_recv()
+    total = z_vectors[0]
+    for other in range(1, place.outer):
+        total = total + z_vectors[other]
+    passed_vector[2] = total
+    y_vectors[place.dp] = total
+    vector_y = [
+        copies.start(
+            passed_vector.at[2], y_vectors.at[place.dp], {"dp": lax.rem(place.dp + other, dp)}
+        )
+        for other in range(1, dp)
+    ]
+    sums[:, share:] = in_tree.result()
+    for copy in vector_y:
+        copy.wait_recv()
+    total = y_vectors[0]
+    for other in range(1, dp):
+        total = total + y_vectors[other]
+    totals[...] = total
+    early.finish()
+    late.finish()
+    copies.finish()
+
+
+def compute_all(
+    row, columns, cosines, sines, norms, up_bias, qkv_bias, width, units, share, ctx, dp, tp, owned
+):
     f32, bf16 = jnp.float32, jnp.bfloat16
     length = row.shape[0]
+    outer, rows = ctx // INNER, length // ctx
+    padded = owned + -owned % 16
+    early_width = 2 * units + -2 * units % 128
+    late_width = 4 * HD
+    slot = 3 * HD + units
+    slot += -slot % 128
+    lines = 5 * width // 128 + tp * ctx * slot // 128
+    lines += -lines % 8
     vmem = pl.BlockSpec(memory_space=pltpu.VMEM)
+    anywhere = pl.BlockSpec(memory_space=pl.ANY)
+    tree = [
+        pltpu.VMEM((tp, length, share), bf16),
+        pltpu.VMEM((length, share), bf16),
+        pltpu.VMEM((outer, rows, share), bf16),
+        pltpu.VMEM((outer, rows, share), bf16),
+        pltpu.VMEM((outer - 1, rows, share), bf16),
+        pltpu.VMEM((outer - 1, rows, share), bf16),
+    ]
+
+    def exchange(block_width):
+        return [
+            pltpu.VMEM((dp, ctx, padded, block_width), bf16),
+            pltpu.VMEM((dp - 1, ctx, padded, block_width), bf16),
+            pltpu.VMEM((ctx, padded, block_width), bf16),
+        ]
+
+    count = 2 * (3 * outer - 1) + 2 * (dp - 1 + ctx - 1) + 2 + (outer - 1) + (dp - 1)
+    vector = (lines, 128)
     return pl.pallas_call(
-        functools.partial(compute_kernel, width, units, share),
+        functools.partial(compute_kernel, width, units, share, ctx, dp, tp, owned),
         out_shape=(
-            jax.ShapeDtypeStruct((width // share, length, 2 * share), bf16),
-            jax.ShapeDtypeStruct(columns.shape, bf16),
-            jax.ShapeDtypeStruct((4, width), f32),
-            jax.ShapeDtypeStruct((1, units), f32),
-            jax.ShapeDtypeStruct((1, 3 * HD), f32),
+            jax.ShapeDtypeStruct((rows, 2 * share), f32),
+            jax.ShapeDtypeStruct((ctx, padded, early_width), bf16),
+            jax.ShapeDtypeStruct((ctx, padded, late_width), bf16),
+            jax.ShapeDtypeStruct(vector, f32),
         ),
         in_specs=[vmem] * 7,
-        out_specs=(vmem,) * 5,
+        out_specs=(vmem, anywhere, anywhere, vmem),
         scratch_shapes=[
-            pltpu.VMEM((length, width), f32),
+            pltpu.VMEM((4, width), f32),
+            pltpu.VMEM((1, slot), f32),
+            pltpu.VMEM((length, 1), f32),
             pltpu.VMEM((length, 1), f32),
             pltpu.VMEM((length, width), bf16),
             pltpu.VMEM((length, width), bf16),
@@ -227,8 +488,25 @@
             pltpu.VMEM((HD, length), f32),
             pltpu.VMEM((length, 3 * HD), bf16),
             pltpu.VMEM((length, 128), bf16),
+        ]
+        + tree
+        + tree
+        + exchange(early_width)
+        + exchange(late_width)
+        + [
+            pltpu.VMEM(vector, f32),
+            pltpu.VMEM(vector, f32),
+            pltpu.VMEM(vector, f32),
+            pltpu.VMEM((3,) + vector, f32),
+            pltpu.VMEM((outer,) + vector, f32),
+            pltpu.VMEM((dp,) + vector, f32),
+            pltpu.SemaphoreType.DMA((count,)),
+            pltpu.SemaphoreType.DMA((count,)),
+            pltpu.SemaphoreType.DMA((2,)),
         ],
-        compiler_params=pltpu.CompilerParams(vmem_limit_bytes=56 * 2**20),
+        compiler_params=pltpu.CompilerParams(
+            collective_id=1, has_side_effects=True, vmem_limit_bytes=60 * 2**20
+        ),
     )(row, columns, cosines, sines, norms, up_bias, qkv_bias)
 
 
@@ -358,185 +636,6 @@
         ],
         compiler_params=pltpu.CompilerParams(collective_id=0, has_side_effects=True),
     )(packed, blocks)
-
-
-def reduce_kernel(
-    ctx,
-    dp,
-    tp,
-    partial,
-    grads,
-    vectors,
-    sums,
-    own_grads,
-    totals,
-    from_core,
-    to_x,
-    from_x,
-    to_z,
-    from_z,
-    from_y,
-    summed,
-    core_vector,
-    x_vector,
-    passed_vector,
-    z_vectors,
-    y_vectors,
-    send_sems,
-    recv_sems,
-    local_sem,
-):
-    f32, bf16 = jnp.float32, jnp.bfloat16
-    my_ctx, my_dp, my_tp = lax.axis_index("ctx"), lax.axis_index("dp"), lax.axis_index("tp")
-    outer = ctx // INNER
-    my_z, my_x = my_ctx // INNER, lax.rem(my_ctx, INNER)
-    rows = sums.shape[0]
-    greet(ctx, dp, tp, my_ctx, my_dp, my_tp)
-    copies = Copies(send_sems, recv_sems)
-    partner = {"ctx": my_z * INNER + (INNER - 1 - my_x)}
-    sibling = {"tp": tp - 1 - my_tp}
-    other_core = tp - 1 - my_tp
-
-    def group(step):
-        first = lax.rem(my_z + step, outer) * INNER * rows
-        return pl.ds(pl.multiple_of(first, rows), INNER * rows)
-
-    def token_rows(step, x):
-        first = (lax.rem(my_z + step, outer) * INNER + x) * rows
-        return pl.ds(pl.multiple_of(first, rows), rows)
-
-    vector_core = copies.start(vectors, core_vector, sibling)
-    order = list(range(1, outer)) + [0]
-    over_core = {}
-    for step in order:
-        here = group(step)
-        over_core[step] = copies.start(
-            partial.at[other_core, here], from_core.at[here], sibling
-        )
-    over_y = []
-    for other in range(1, dp):
-        target = lax.rem(my_dp + other, dp)
-        over_y.append(copies.start(grads.at[target], from_y.at[other - 1], {"dp": target}))
-
-    over_x = {}
-    for step in order:
-        over_core[step].wait_recv()
-        there = token_rows(step, INNER - 1 - my_x)
-        to_x[step] = (
-            partial[my_tp, there, :].astype(f32) + from_core[there, :].astype(f32)
-        ).astype(bf16)
-        over_x[step] = copies.start(to_x.at[step], from_x.at[step], partner)
-
-    vector_core.wait_recv()
-    passed_vector[0] = vectors[...] + core_vector[...]
-    vector_x = copies.start(passed_vector.at[0], x_vector, partner)
-
-    def own_sum(step):
-        here = token_rows(step, my_x)
-        local = partial[my_tp, here, :].astype(f32) + from_core[here, :].astype(f32)
-        return local + from_x[step].astype(f32)
-
-    over_z = {}
-    for step in range(1, outer):
-        over_x[step].wait_recv()
-        to_z[step - 1] = own_sum(step).astype(bf16)
-        target = lax.rem(my_z + step, outer) * INNER + my_x
-        over_z[step] = copies.start(to_z.at[step - 1], from_z.at[step - 1], {"ctx": target})
-
-    vector_x.wait_recv()
-    passed_vector[1] = passed_vector[0] + x_vector[...]
-    z_vectors[my_z] = passed_vector[1]
-    vector_z = []
-    for step in range(1, outer):
-        target = lax.rem(my_z + step, outer) * INNER + my_x
-        vector_z.append(
-            copies.start(passed_vector.at[1], z_vectors.at[my_z], {"ctx": target})
-        )
-
-    for copy in over_y:
-        copy.wait_recv()
-    over_ctx = []
-    for step in list(range(1, ctx)) + [0]:
-        target = lax.rem(my_ctx + step, ctx)
-        total = grads[my_dp, target].astype(f32)
-        for other in range(1, dp):
-            total = total + from_y[other - 1, target].astype(f32)
-        summed[step] = total.astype(bf16)
-        if step > 0:
-            over_ctx.append(
-                copies.start(summed.at[step], own_grads.at[my_ctx], {"ctx": target})
-            )
-    own = pltpu.make_async_copy(summed.at[0], own_grads.at[my_ctx], local_sem)
-    own.start()
-
-    for copy in vector_z:
-        copy.wait_recv()
-    total = z_vectors[0]
-    for place in range(1, outer):
-        total = total + z_vectors[place]
-    passed_vector[2] = total
-    y_vectors[my_dp] = total
-    vector_y = []
-    for other in range(1, dp):
-        target = {"dp": lax.rem(my_dp + other, dp)}
-        vector_y.append(copies.start(passed_vector.at[2], y_vectors.at[my_dp], target))
-
-    over_x[0].wait_recv()
-    result = own_sum(0)
-    for step in range(1, outer):
-        over_z[step].wait_recv()
-        result = result + from_z[step - 1].astype(f32)
-    sums[...] = result
-    for copy in vector_y:
-        copy.wait_recv()
-    total = y_vectors[0]
-    for place in range(1, dp):
-        total = total + y_vectors[place]
-    totals[...] = total
-    for copy in over_ctx:
-        copy.wait_recv()
-    copies.finish()
-    own.wait()
-
-
-def reduce_all(partial, grads, vectors, dp, ctx, tp):
-    outer = ctx // INNER
-    rows, width = partial.shape[1] // ctx, partial.shape[2]
-    block = grads.shape[2:]
-    bf16 = jnp.bfloat16
-    count = outer + (dp - 1) + outer + (outer - 1) + (ctx - 1)
-    count += 2 + (outer - 1) + (dp - 1)
-    vmem = pl.BlockSpec(memory_space=pltpu.VMEM)
-    return pl.pallas_call(
-        functools.partial(reduce_kernel, ctx, dp, tp),
-        out_shape=(
-            jax.ShapeDtypeStruct((rows, width), jnp.float32),
-            jax.ShapeDtypeStruct((ctx,) + block, bf16),
-            jax.ShapeDtypeStruct(vectors.shape, jnp.float32),
-        ),
-        in_specs=[vmem] * 3,
-        out_specs=(vmem, pl.BlockSpec(memory_space=pl.ANY), vmem),
-        scratch_shapes=[
-            pltpu.VMEM(partial.shape[1:], bf16),
-            pltpu.VMEM((outer, rows, width), bf16),
-            pltpu.VMEM((outer, rows, width), bf16),
-            pltpu.VMEM((outer - 1, rows, width), bf16),
-            pltpu.VMEM((outer - 1, rows, width), bf16),
-            pltpu.VMEM((dp - 1, ctx) + block, bf16),
-            pltpu.VMEM((ctx,) + block, bf16),
-            pltpu.VMEM(vectors.shape, jnp.float32),
-            pltpu.VMEM(vectors.shape, jnp.float32),
-            pltpu.VMEM((3,) + vectors.shape, jnp.float32),
-            pltpu.VMEM((outer,) + vectors.shape, jnp.float32),
-            pltpu.VMEM((dp,) + vectors.shape, jnp.float32),
-            pltpu.SemaphoreType.DMA((count,)),
-            pltpu.SemaphoreType.DMA((count,)),
-            pltpu.SemaphoreType.DMA,
-        ],
-        compiler_params=pltpu.CompilerParams(
-            collective_id=1, has_side_effects=True, vmem_limit_bytes=48 * 2**20
-        ),
-    )(partial, grads, vectors)
 
 
 def on_device(
@@ -591,57 +690,40 @@
     qkv_bias = lax.dynamic_index_in_dim(qkv_bias, my_ctx, 1, keepdims=False).reshape(-1)
     up_bias = lax.dynamic_slice_in_dim(b_up, my_ctx * units, units, 0)
 
-    cosine_table, sine_table = angle_tables(0, length)
-    rest = jnp.zeros((length, HD - ROT), f32)
-    cosines = jnp.concatenate([cosine_table, cosine_table, rest + 1.0], axis=-1)
-    sines = jnp.concatenate([sine_table, sine_table, rest], axis=-1)
+    cosines, sines = angle_tables(length)
     norms = jnp.stack([gain_one, bias_one, gain_two, bias_two])
-    partial, grads, norm_grads, grad_b_up, grad_b_qkv = compute_all(
+    sums, early, late, total = compute_all(
         row,
         columns,
-        jnp.concatenate([cosines, cosines], axis=-1),
-        jnp.concatenate([sines, sines], axis=-1),
+        jnp.asarray(cosines),
+        jnp.asarray(sines),
         norms,
         up_bias[None],
         qkv_bias[None],
         width,
         units,
         share,
-    )
-
-    grads = grads.reshape(dp, ctx, owned, -1)
-    grads = jnp.pad(grads, ((0, 0), (0, 0), (0, pad_rows), (0, pad_width)))
-
-    grad_bias = jnp.sum(cotangent[0].astype(f32), axis=0) * (my_tp == 0).astype(f32)
-    place = (jnp.arange(tp)[:, None] == my_tp) & (jnp.arange(ctx)[None, :] == my_ctx)
-    local = jnp.concatenate([grad_b_qkv[0], grad_b_up[0]])
-    spread = jnp.where(place[:, :, None], local, 0.0)
-    vectors = jnp.concatenate(
-        [
-            norm_grads.reshape(-1),
-            grad_bias,
-            spread.reshape(-1),
-        ]
-    )
-    vector_size = vectors.shape[0]
-    vectors = jnp.pad(vectors, (0, -vector_size % 1024)).reshape(-1, 128)
-    sums, own, total = reduce_all(partial, grads, vectors, dp, ctx, tp)
+        ctx,
+        dp,
+        tp,
+        owned,
+    )
     branch_share, input_share = sums[:, :share], sums[:, share:]
-    own = own[:, :owned, :block_width].astype(f32)
-    own_down = own[:, :, :units].transpose(1, 0, 2).reshape(owned, -1)
-    own_out = own[:, :, units : units + head_width].transpose(1, 0, 2)
-    own_out = own_out.reshape(owned, -1)[:, : heads * HD]
-    first = units + head_width
-    own_up = own[:, :, first : first + units].transpose(1, 0, 2).reshape(owned, -1)
-    own_qkv = own[:, :, first + units :].reshape(ctx, owned, 3, head_width)
-    own_qkv = own_qkv.transpose(1, 2, 0, 3).reshape(owned, 3, ctx * head_width)
-    own_qkv = own_qkv[:, :, : heads * HD]
-    total = total.reshape(-1)[:vector_size]
-    spread = total[5 * width :].reshape(tp, ctx, -1)
+    early, late = early[:, :owned].astype(f32), late[:, :owned].astype(f32)
+    own_down = early[:, :, :units].transpose(1, 0, 2).reshape(owned, -1)
+    own_up = early[:, :, units : 2 * units].transpose(1, 0, 2).reshape(owned, -1)
+    own_out = late[:, :, :HD].transpose(1, 0, 2).reshape(owned, -1)[:, : heads * HD]
+    own_qkv = late[:, :, HD:].reshape(ctx, owned, 3, HD).transpose(1, 2, 0, 3)
+    own_qkv = own_qkv.reshape(owned, 3, ctx * HD)[:, :, : heads * HD]
+    total = total.reshape(-1)
+    slot = 3 * HD + units
+    slot += -slot % 128
+    spread = total[5 * width : 5 * width + tp * ctx * slot].reshape(tp, ctx, slot)
+
     spread = lax.dynamic_index_in_dim(spread, my_tp, 0, keepdims=False)
     sum_b_qkv = spread[:, : 3 * head_width].reshape(ctx, 3, head_width).transpose(1, 0, 2)
     sum_b_qkv = sum_b_qkv.reshape(3, -1)[:, : heads * HD]
-    sum_b_up = spread[:, 3 * head_width :].reshape(-1)
+    sum_b_up = spread[:, 3 * head_width : 3 * head_width + units].reshape(-1)
 
     start = my_tp * share
     token_share = lax.dynamic_slice_in_dim(inputs[0], start, share, 1).astype(f32)

time: 133 us -> 124 us (0.932)
  local copies, waits for them, and re-layouts: 21.5 us -> 16.5 us
  other arithmetic: 6.17 us -> 4.29 us
    concatenate x2 -> x0, local copies, waits for them, and re-layouts: 3.69 us -> none  [the longest x1 1.95 us: on_device(): jnp.concatenate([cosines, cosines], axis=-1)]
    unnamed x22, local copies, waits for them, and re-layouts: 3.13 us -> 0.04 us
    sin x1 -> x0, other arithmetic: 1.88 us -> none  [angle_tables(): return (jnp.cos(angles), jnp.sin(angles))]
    slice x5, local copies, waits for them, and re-layouts: 1.54 us -> 3.21 us  [the longest x1 1.04 us: on_device(): own_qkv = late[:, :, HD:].reshape(ctx, owned, 3, HD).transpose(1, 2, 0, 3)]
    pallas_call x2 -> x1, Pallas kernels: 61.5 us -> 60.6 us  [compute_all(): pl.pallas_call(functools.partial(compute_kernel, width, units, share, ctx...]
    reshape x8 -> x7, local copies, waits for them, and re-layouts: 3.63 us -> 2.91 us  [the longest x1 0.86 us: on_device(): own_down = early[:, :, :units].transpose(1, 0, 2).reshape(owned, -1)]
where the time goes in v4:
time: 124 us
  Pallas kernels  102 us (82%)
  local copies, waits for them, and re-layouts  16.5 us (13%)
  other arithmetic  4.29 us (3%)
    pallas_call x1, Pallas kernels, compute_all(): pl.pallas_call(functools.partial(compute_kernel, width, units, share, ctx...  60.6 us
    pallas_call x1, Pallas kernels, gather_all(): pl.pallas_call(functools.partial(gather_kernel, ctx, dp, tp), out_shape=(...  41.7 us

profile of v4, /device:TPU:0, one launch (start us, length us, event | category | flops | bytes accessed | tf_op | source)
XLA Modules:
  0.0 124.1 jit_solution(17967122234691130729)
XLA Ops:
  0.6 0.0 copy-start.4
  0.7 0.0 copy-start.10
  0.7 0.0 copy-start.2
  0.7 0.0 copy-start.1
  0.7 1.4 %dynamic_slice.21 = f32[192]{0:T(256)} dynamic-slice(f32[1536]{0:T(1024)} %param.27, s32[]{:T(128)S(6)} %select_n.17), dynamic_slice_sizes={192} | dynamic-slice | bytes 1540 | tf_op jit(solution)/shard_map/dynamic_slice | solution.py:691
  2.1 0.7 pad.14
  2.8 0.1 reshape.102
  2.9 0.6 broadcast_in_dim_reshape.3.qkv_bias
  3.5 0.0 copy-start.5
  3.5 0.0 copy-start.6
  3.5 0.0 copy-start.7
  3.5 0.0 copy-start.8
  3.5 1.2 reshape.96
  4.7 1.1 reshape.98
  5.8 0.1 copy_bitcast_fusion.1
  5.9 0.9 pad.13
  6.8 0.2 reshape.99
  7.0 0.3 copy.55
  7.3 0.2 reshape.100
  7.5 0.0 copy-done.4
  7.6 0.1 reshape.97
  7.7 1.0 pad_maximum_fusion.blocks
  8.7 0.0 copy-done.10
  8.7 0.1 broadcast_in_dim.16
  8.8 0.0 copy-done.2
  8.8 0.0 copy-done.1
  8.8 0.8 pad_maximum_fusion.1.packed
  9.6 0.0 copy-start.9
  9.6 41.7 %shard_map.255 = (bf16[1024,1664]{1,0:T(8,128)(2,1)}, bf16[2,8,48,640]{3,2,1,0:T(8,128)(2,1)}) custom-call(bf16[128,1664]{1,0:T(8,128)(2,1)} %pad_maximum_fusion.1.packed, bf16[8,48,640]{2,1,0:T(8,128)(2,1)} %pad_maximum_fusion.blocks), custom_call_target="tpu_custom_call" | custom-call | tf_op jit(solution)/shard_map/pallas_call | solution.py:624
  51.3 0.0 copy-done.5
  51.4 0.0 copy-done.6
  51.4 0.0 copy-done.7
  51.4 0.0 copy-done.8
  51.4 0.6 pad_maximum_fusion.2.norms
  52.0 60.6 %shard_map.256 = (f32[128,768]{1,0:T(8,128)}, bf16[8,48,384]{2,1,0:T(8,128)(2,1)}, bf16[8,48,256]{2,1,0:T(8,128)(2,1)}, f32[80,128]{1,0:T(8,128)}) custom-call(bf16[1024,1664]{1,0:T(8,128)(2,1)} %get-tuple-element.19.row, bf16[768,640]{1,0:T(8,128)(2,1)} %bitcast.54, f32[1024,128]{1,0:T(8,128)} %constant.38.clone.cosines, f32[1024,128]{1,0:T(8,128)} %constant.39.clone.sines, ...), custom_call_target="tpu_custom_call" | custom-call | tf_op jit(solution)/shard_map/pallas_call | solution.py:463
  112.6 0.0 copy-start.3
  112.7 0.0 copy-done.9
  112.7 0.1 dynamic_slice.23
  112.8 1.8 %fusion = (f32[1,128,384]{2,1,0:T(8,128)}, f32[1,128,384]{2,1,0:T(8,128)}) fusion(f32[128,768]{1,0:T(8,128)} %get-tuple-element.21, bf16[1,128,768]{2,1,0:T(8,128)(2,1)S(1)} %copy-done.1, s32[]{:T(128)S(6)} %select_n.16, f32[384]{0:T(512)S(1)} %dynamic_slice.23, bf16[1,128,768]{2,1,0:T(8,128)(2,1)S(1)} %copy-done.2), kind=kLoop, calls=%fused_computation.7 | loop fusion | flops 245760 | bytes 984580 | tf_op jit(solution)/shard_map/broadcast_in_dim | solution.py:736
  114.6 0.8 slice.79
  115.3 0.1 fusion.3
  115.4 0.1 reshape.106
  115.5 0.1 reshape.107
  115.6 0.6 slice.92
  116.2 0.7 reshape.110
  116.8 1.4 %slice_bitcast_fusion.3 = (f32[768]{0:T(1024)}, f32[768]{0:T(1024)}, f32[768]{0:T(1024)}, f32[768]{0:T(1024)}, f32[768]{0:T(1024)}) fusion(f32[80,128]{1,0:T(8,128)} %get-tuple-element.22), kind=kLoop, calls=%fused_computation.16 | loop fusion | bytes 30720 | tf_op jit(solution)/shard_map/slice | solution.py:744
  118.2 1.0 slice.89
  119.3 0.2 reshape.103
  119.5 0.3 copy.45
  119.9 0.0 copy-start
  119.9 0.2 reshape.104
  120.1 0.7 slice.90
  120.8 0.0 copy-done.3
  120.8 0.2 slice_bitcast_fusion
  121.0 0.2 copy.48
  121.2 0.9 reshape.109
  122.1 0.2 copy.49
  122.3 0.9 reshape.111
  123.2 0.0 copy-done
  123.2 0.1 copy.47
  123.3 0.1 reshape.108
  123.4 0.6 slice.94
  (14 shorter events, 0.2 us)
Async XLA Ops:
  0.6 6.9 %copy-start.4 = (bf16[48,384]{1,0:T(8,128)(2,1)S(1)}, bf16[48,384]{1,0:T(8,128)(2,1)}, u32[]{:S(2)}) copy-start(bf16[48,384]{1,0:T(8,128)(2,1)} %param.24) | copy-start | bytes 110596
  0.7 8.0 %copy-start.10 = (s32[1,128]{1,0:T(1,128)S(1)}, s32[1,128]{1,0:T(1,128)}, u32[]{:S(2)}) copy-start(s32[1,128]{1,0:T(1,128)} %param.17) | copy-start | bytes 1540
  0.7 8.1 %copy-start.2 = (bf16[1,128,768]{2,1,0:T(8,128)(2,1)S(1)}, bf16[1,128,768]{2,1,0:T(8,128)(2,1)}, u32[]{:S(2)}) copy-start(bf16[1,128,768]{2,1,0:T(8,128)(2,1)} %param.16) | copy-start | bytes 589828
  0.7 8.1 %copy-start.1 = (bf16[1,128,768]{2,1,0:T(8,128)(2,1)S(1)}, bf16[1,128,768]{2,1,0:T(8,128)(2,1)}, u32[]{:S(2)}) copy-start(bf16[1,128,768]{2,1,0:T(8,128)(2,1)} %param.29) | copy-start | bytes 589828
  3.5 47.8 %copy-start.5 = (f32[768]{0:T(1024)S(1)}, f32[768]{0:T(1024)}, u32[]{:S(2)}) copy-start(f32[768]{0:T(1024)} %param.18) | copy-start | bytes 9220
  3.5 47.8 %copy-start.6 = (f32[768]{0:T(1024)S(1)}, f32[768]{0:T(1024)}, u32[]{:S(2)}) copy-start(f32[768]{0:T(1024)} %param.19) | copy-start | bytes 9220
  3.5 47.8 %copy-start.7 = (f32[768]{0:T(1024)S(1)}, f32[768]{0:T(1024)}, u32[]{:S(2)}) copy-start(f32[768]{0:T(1024)} %param.20) | copy-start | bytes 9220
  3.5 47.9 %copy-start.8 = (f32[768]{0:T(1024)S(1)}, f32[768]{0:T(1024)}, u32[]{:S(2)}) copy-start(f32[768]{0:T(1024)} %param.21) | copy-start | bytes 9220
  9.6 103.1 %copy-start.9 = (f32[768]{0:T(1024)S(1)}, f32[768]{0:T(1024)}, u32[]{:S(2)}) copy-start(f32[768]{0:T(1024)} %param.25) | copy-start | bytes 9220
  112.6 8.1 %copy-start.3 = (bf16[8,48,384]{2,1,0:T(8,128)(2,1)S(1)}, bf16[8,48,384]{2,1,0:T(8,128)(2,1)}, u32[]{:S(2)}) copy-start(bf16[8,48,384]{2,1,0:T(8,128)(2,1)} %get-tuple-element.24) | copy-start | bytes 884740
  119.9 3.3 %copy-start = (bf16[8,48,256]{2,1,0:T(8,128)(2,1)S(1)}, bf16[8,48,256]{2,1,0:T(8,128)(2,1)}, u32[]{:S(2)}) copy-start(bf16[8,48,256]{2,1,0:T(8,128)(2,1)} %get-tuple-element.23) | copy-start | bytes 589828

commit v5 on v4

--- a/solution.py
+++ b/solution.py
@@ -552,11 +552,27 @@
 
 
 def gather_kernel(
-    ctx, dp, tp, packed, blocks, row, columns, send_sems, recv_sems, local_sems
+    ctx,
+    dp,
+    tp,
+    packed,
+    blocks,
+    row,
+    columns,
+    send_sems,
+    recv_sems,
+    line_send,
+    line_recv,
+    x_send,
+    x_recv,
+    core_send,
+    core_recv,
+    local_sems,
 ):
     my_ctx, my_dp, my_tp = lax.axis_index("ctx"), lax.axis_index("dp"), lax.axis_index("tp")
     outer = ctx // INNER
     my_z, my_x = my_ctx // INNER, lax.rem(my_ctx, INNER)
+    other_x = INNER - 1 - my_x
     rows = packed.shape[0]
     half = rows // tp
 
@@ -574,31 +590,92 @@
     greet(ctx, dp, tp, my_ctx, my_dp, my_tp)
     copies = Copies(send_sems, recv_sems)
     mine = packed.at[pl.ds(pl.multiple_of(my_tp * half, half), half)]
-    partner = {"ctx": my_z * INNER + (INNER - 1 - my_x)}
+    partner = {"ctx": my_z * INNER + other_x}
     sibling = {"tp": tp - 1 - my_tp}
-    along = []
+
+    def inside(place):
+        return (place >= 0) & (place < outer)
+
+    def hop(way, step):
+        place = 0 if way > 0 else 1
+        shard = (my_z - way * step) * INNER + my_x
+        return pltpu.make_async_remote_copy(
+            src_ref=mine if step == 0 else piece(shard, my_tp),
+            dst_ref=piece(shard, my_tp),
+            send_sem=line_send.at[place, step],
+            recv_sem=line_recv.at[place, step],
+            device_id={"ctx": (my_z + way) * INNER + my_x},
+            device_id_type=MESH,
+        )
+
+    def hops_on(way, step):
+        return inside(my_z - way * step) & inside(my_z + way)
+
+    def cross(shard_z, own):
+        shard = shard_z * INNER + my_x
+        return pltpu.make_async_remote_copy(
+            src_ref=mine if own else piece(shard, my_tp),
+            dst_ref=piece(shard, my_tp),
+            send_sem=x_send.at[shard_z],
+            recv_sem=x_recv.at[shard_z],
+            device_id=partner,
+            device_id_type=MESH,
+        )
+
+    def to_sibling(shard):
+        return pltpu.make_async_remote_copy(
+            src_ref=piece(shard, my_tp),
+            dst_ref=piece(shard, my_tp),
+            send_sem=core_send.at[shard],
+            recv_sem=core_recv.at[shard],
+            device_id=sibling,
+            device_id_type=MESH,
+        )
+
+    for way in (1, -1):
+
+        @pl.when(hops_on(way, 0))
+        def _(way=way):
+            hop(way, 0).start()
+
+    cross(my_z, True).start()
     for step in range(1, outer):
-        target = lax.rem(my_z + step, outer) * INNER + my_x
-        along.append(copies.start(mine, piece(my_ctx, my_tp), {"ctx": target}))
-    across = [copies.start(mine, piece(my_ctx, my_tp), partner)]
+        for way in (1, -1):
+
+            @pl.when(inside(my_z - way * step))
+            def _(way=way, step=step):
+                hop(way, step - 1).wait_recv()
+                if step < outer - 1:
+
+                    @pl.when(inside(my_z + way))
+                    def _():
+                        hop(way, step).start()
+
+                shard_z = my_z - way * step
+                cross(shard_z, False).start()
+                to_sibling(shard_z * INNER + my_x).start()
+
     exchanged = []
     for step in range(1, ctx):
         target = lax.rem(my_ctx + step, ctx)
         exchanged.append(
             copies.start(blocks.at[target], columns.at[my_dp, my_ctx], {"ctx": target})
         )
-    to_sibling = []
-    for step in range(1, outer):
-        source = lax.rem(my_z + outer - step, outer) * INNER + my_x
-        along[step - 1].wait_recv()
-        across.append(copies.start(piece(source, my_tp), piece(source, my_tp), partner))
-        to_sibling.append(copies.start(piece(source, my_tp), piece(source, my_tp), sibling))
     over_dp = []
     for other in range(1, dp):
         target = {"dp": lax.rem(my_dp + other, dp)}
         over_dp.append(
             copies.start(blocks.at[my_ctx], columns.at[my_dp, my_ctx], target)
         )
+    for step in range(outer):
+        for way in (1, -1) if step > 0 else (1,):
+
+            @pl.when(inside(my_z - way * step))
+            def _(way=way, step=step):
+                shard_z = my_z - way * step
+                cross(shard_z, False).wait_recv()
+                to_sibling(shard_z * INNER + other_x).start()
+
     for step in range(1, ctx):
         source = lax.rem(my_ctx + ctx - step, ctx)
         exchanged[step - 1].wait_recv()
@@ -607,20 +684,29 @@
             over_dp.append(
                 copies.start(columns.at[my_dp, source], columns.at[my_dp, source], target)
             )
-    for step in range(outer):
-        source = lax.rem(my_z + outer - step, outer) * INNER + (INNER - 1 - my_x)
-        across[step].wait_recv()
-        to_sibling.append(copies.start(piece(source, my_tp), piece(source, my_tp), sibling))
-    for copy in over_dp + to_sibling:
+    for step in range(1, ctx):
+        copy = to_sibling(lax.rem(my_ctx + step, ctx))
+        copy.wait_recv()
+        copy.wait_send()
+    for copy in over_dp:
         copy.wait_recv()
     copies.finish()
+    for shard_z in range(outer):
+        cross(shard_z, False).wait_send()
+    for step in range(outer - 1):
+        for way in (1, -1):
+
+            @pl.when(hops_on(way, step))
+            def _(way=way, step=step):
+                hop(way, step).wait_send()
+
     own_row.wait()
     own_block.wait()
 
 
 def gather_all(packed, blocks, dp, ctx, tp):
     outer = ctx // INNER
-    count = (outer - 1) + outer + (ctx - 1) + (2 * outer - 1) + ctx * (dp - 1)
+    count = (ctx - 1) + ctx * (dp - 1)
     return pl.pallas_call(
         functools.partial(gather_kernel, ctx, dp, tp),
         out_shape=(
@@ -632,6 +718,12 @@
         scratch_shapes=[
             pltpu.SemaphoreType.DMA((count,)),
             pltpu.SemaphoreType.DMA((count,)),
+            pltpu.SemaphoreType.DMA((2, outer - 1)),
+            pltpu.SemaphoreType.DMA((2, outer - 1)),
+            pltpu.SemaphoreType.DMA((outer,)),
+            pltpu.SemaphoreType.DMA((outer,)),
+            pltpu.SemaphoreType.DMA((ctx,)),
+            pltpu.SemaphoreType.DMA((ctx,)),
             pltpu.SemaphoreType.DMA((2,)),
         ],
         compiler_params=pltpu.CompilerParams(collective_id=0, has_side_effects=True),

time: 124 us -> 124 us (level)
  no operation moved by 1% of the time
where the time goes in v5:
time: 124 us
  Pallas kernels  102 us (82%)
  local copies, waits for them, and re-layouts  16.5 us (13%)
  other arithmetic  4.29 us (3%)
    pallas_call x1, Pallas kernels, compute_all(): pl.pallas_call(functools.partial(compute_kernel, width, units, share, ctx...  59.4 us
    pallas_call x1, Pallas kernels, gather_all(): pl.pallas_call(functools.partial(gather_kernel, ctx, dp, tp), out_shape=(...  42.9 us

profile of v5, /device:TPU:0, one launch (start us, length us, event | category | flops | bytes accessed | tf_op | source)
XLA Modules:
  0.0 124.0 jit_solution(4344359306381610872)
XLA Ops:
  0.6 0.0 copy-start.4
  0.7 0.0 copy-start.10
  0.7 0.0 copy-start.2
  0.7 0.0 copy-start.1
  0.7 1.4 %dynamic_slice.21 = f32[192]{0:T(256)} dynamic-slice(f32[1536]{0:T(1024)} %param.27, s32[]{:T(128)S(6)} %select_n.17), dynamic_slice_sizes={192} | dynamic-slice | bytes 1540 | tf_op jit(solution)/shard_map/dynamic_slice | solution.py:783
  2.1 0.7 pad.14
  2.8 0.1 reshape.102
  2.9 0.6 broadcast_in_dim_reshape.3.qkv_bias
  3.5 0.0 copy-start.5
  3.5 0.0 copy-start.6
  3.5 0.0 copy-start.7
  3.5 0.0 copy-start.8
  3.5 1.2 reshape.96
  4.7 1.1 reshape.98
  5.8 0.1 copy_bitcast_fusion.1
  5.9 0.9 pad.13
  6.8 0.2 reshape.99
  7.0 0.3 copy.55
  7.3 0.2 reshape.100
  7.5 0.0 copy-done.4
  7.6 0.1 reshape.97
  7.7 1.0 pad_maximum_fusion.blocks
  8.7 0.0 copy-done.10
  8.7 0.1 broadcast_in_dim.16
  8.8 0.0 copy-done.2
  8.8 0.0 copy-done.1
  8.8 0.8 pad_maximum_fusion.1.packed
  9.6 0.0 copy-start.9
  9.6 42.9 %shard_map.255 = (bf16[1024,1664]{1,0:T(8,128)(2,1)}, bf16[2,8,48,640]{3,2,1,0:T(8,128)(2,1)}) custom-call(bf16[128,1664]{1,0:T(8,128)(2,1)} %pad_maximum_fusion.1.packed, bf16[8,48,640]{2,1,0:T(8,128)(2,1)} %pad_maximum_fusion.blocks), custom_call_target="tpu_custom_call" | custom-call | tf_op jit(solution)/shard_map/pallas_call | solution.py:710
  52.5 0.0 copy-done.5
  52.6 0.0 copy-done.6
  52.6 0.0 copy-done.7
  52.6 0.0 copy-done.8
  52.6 0.6 pad_maximum_fusion.2.norms
  53.2 59.4 %shard_map.256 = (f32[128,768]{1,0:T(8,128)}, bf16[8,48,384]{2,1,0:T(8,128)(2,1)}, bf16[8,48,256]{2,1,0:T(8,128)(2,1)}, f32[80,128]{1,0:T(8,128)}) custom-call(bf16[1024,1664]{1,0:T(8,128)(2,1)} %get-tuple-element.19.row, bf16[768,640]{1,0:T(8,128)(2,1)} %bitcast.54, f32[1024,128]{1,0:T(8,128)} %constant.38.clone.cosines, f32[1024,128]{1,0:T(8,128)} %constant.39.clone.sines, ...), custom_call_target="tpu_custom_call" | custom-call | tf_op jit(solution)/shard_map/pallas_call | solution.py:463
  112.6 0.0 copy-start.3
  112.6 0.0 copy-done.9
  112.7 0.1 dynamic_slice.23
  112.7 1.8 %fusion = (f32[1,128,384]{2,1,0:T(8,128)}, f32[1,128,384]{2,1,0:T(8,128)}) fusion(f32[128,768]{1,0:T(8,128)} %get-tuple-element.21, bf16[1,128,768]{2,1,0:T(8,128)(2,1)S(1)} %copy-done.1, s32[]{:T(128)S(6)} %select_n.16, f32[384]{0:T(512)S(1)} %dynamic_slice.23, bf16[1,128,768]{2,1,0:T(8,128)(2,1)S(1)} %copy-done.2), kind=kLoop, calls=%fused_computation.7 | loop fusion | flops 245760 | bytes 984580 | tf_op jit(solution)/shard_map/broadcast_in_dim | solution.py:828
  114.5 0.8 slice.79
  115.3 0.1 fusion.3
  115.4 0.1 reshape.106
  115.5 0.1 reshape.107
  115.6 0.6 slice.92
  116.2 0.7 reshape.110
  116.8 1.4 %slice_bitcast_fusion.3 = (f32[768]{0:T(1024)}, f32[768]{0:T(1024)}, f32[768]{0:T(1024)}, f32[768]{0:T(1024)}, f32[768]{0:T(1024)}) fusion(f32[80,128]{1,0:T(8,128)} %get-tuple-element.22), kind=kLoop, calls=%fused_computation.16 | loop fusion | bytes 30720 | tf_op jit(solution)/shard_map/slice | solution.py:836
  118.2 1.0 slice.89
  119.3 0.2 reshape.103
  119.5 0.3 copy.45
  119.9 0.0 copy-start
  119.9 0.2 reshape.104
  120.1 0.7 slice.90
  120.8 0.0 copy-done.3
  120.8 0.2 slice_bitcast_fusion
  121.0 0.2 copy.48
  121.2 0.9 reshape.109
  122.1 0.2 copy.49
  122.3 0.9 reshape.111
  123.2 0.0 copy-done
  123.2 0.1 copy.47
  123.3 0.1 reshape.108
  123.4 0.6 slice.94
  (14 shorter events, 0.2 us)
Async XLA Ops:
  0.6 6.9 %copy-start.4 = (bf16[48,384]{1,0:T(8,128)(2,1)S(1)}, bf16[48,384]{1,0:T(8,128)(2,1)}, u32[]{:S(2)}) copy-start(bf16[48,384]{1,0:T(8,128)(2,1)} %param.24) | copy-start | bytes 110596
  0.7 8.0 %copy-start.10 = (s32[1,128]{1,0:T(1,128)S(1)}, s32[1,128]{1,0:T(1,128)}, u32[]{:S(2)}) copy-start(s32[1,128]{1,0:T(1,128)} %param.17) | copy-start | bytes 1540
  0.7 8.1 %copy-start.2 = (bf16[1,128,768]{2,1,0:T(8,128)(2,1)S(1)}, bf16[1,128,768]{2,1,0:T(8,128)(2,1)}, u32[]{:S(2)}) copy-start(bf16[1,128,768]{2,1,0:T(8,128)(2,1)} %param.16) | copy-start | bytes 589828
  0.7 8.1 %copy-start.1 = (bf16[1,128,768]{2,1,0:T(8,128)(2,1)S(1)}, bf16[1,128,768]{2,1,0:T(8,128)(2,1)}, u32[]{:S(2)}) copy-start(bf16[1,128,768]{2,1,0:T(8,128)(2,1)} %param.29) | copy-start | bytes 589828
  3.5 49.0 %copy-start.5 = (f32[768]{0:T(1024)S(1)}, f32[768]{0:T(1024)}, u32[]{:S(2)}) copy-start(f32[768]{0:T(1024)} %param.18) | copy-start | bytes 9220
  3.5 49.0 %copy-start.6 = (f32[768]{0:T(1024)S(1)}, f32[768]{0:T(1024)}, u32[]{:S(2)}) copy-start(f32[768]{0:T(1024)} %param.19) | copy-start | bytes 9220
  3.5 49.0 %copy-start.7 = (f32[768]{0:T(1024)S(1)}, f32[768]{0:T(1024)}, u32[]{:S(2)}) copy-start(f32[768]{0:T(1024)} %param.20) | copy-start | bytes 9220
  3.5 49.1 %copy-start.8 = (f32[768]{0:T(1024)S(1)}, f32[768]{0:T(1024)}, u32[]{:S(2)}) copy-start(f32[768]{0:T(1024)} %param.21) | copy-start | bytes 9220
  9.6 103.0 %copy-start.9 = (f32[768]{0:T(1024)S(1)}, f32[768]{0:T(1024)}, u32[]{:S(2)}) copy-start(f32[768]{0:T(1024)} %param.25) | copy-start | bytes 9220
  112.6 8.1 %copy-start.3 = (bf16[8,48,384]{2,1,0:T(8,128)(2,1)S(1)}, bf16[8,48,384]{2,1,0:T(8,128)(2,1)}, u32[]{:S(2)}) copy-start(bf16[8,48,384]{2,1,0:T(8,128)(2,1)} %get-tuple-element.24) | copy-start | bytes 884740
  119.9 3.3 %copy-start = (bf16[8,48,256]{2,1,0:T(8,128)(2,1)S(1)}, bf16[8,48,256]{2,1,0:T(8,128)(2,1)}, u32[]{:S(2)}) copy-start(bf16[8,48,256]{2,1,0:T(8,128)(2,1)} %get-tuple-element.23) | copy-start | bytes 589828
